TPU v7x, 32 devices: a whole 2x2x4 slice. The times are simulated.
32 devices in a mesh: dp: 4 (over z), zero: 8 (over y, x, core).
Axes of the slice: x: 2, y: 2, z: 4, core: 2. Of those that a mesh axis runs over, the one named last changes fastest.
Arguments:
- images: bfloat16 [160, 197, 768], P(('dp', 'zero')), may hold values from -6 to 6
- cotangent: bfloat16 [160, 197, 768], P(('dp', 'zero')), may hold values from -6 to 6
- counts: int32 [32], P(('dp', 'zero')), may hold values from 3 to 5, as said below
- master_qkv: float32 [768, 2304], P('zero'), may hold values from -0.21875 to 0.21875
- master_proj: float32 [768, 768], P('zero'), may hold values from -0.875 to 0.875
- master_fc1: float32 [768, 3072], P('zero'), may hold values from -0.21875 to 0.21875
- master_fc2: float32 [3072, 768], P('zero'), may hold values from -0.109375 to 0.109375
- master_vectors: float32 [12, 768], P(None, 'zero'), may hold values from -1 to 1.6
- first_qkv: float32 [768, 2304], P('zero'), may hold values from -56 to 56
- first_proj: float32 [768, 768], P('zero'), may hold values from -56 to 56
- first_fc1: float32 [768, 3072], P('zero'), may hold values from -56 to 56
- first_fc2: float32 [3072, 768], P('zero'), may hold values from -56 to 56
- first_vectors: float32 [12, 768], P(None, 'zero'), may hold values from -112 to 112
- second_qkv: float32 [768, 2304], P('zero'), may hold values from 7.88 to 31.52
- second_proj: float32 [768, 768], P('zero'), may hold values from 7.88 to 31.52
- second_fc1: float32 [768, 3072], P('zero'), may hold values from 7.88 to 31.52
- second_fc2: float32 [3072, 768], P('zero'), may hold values from 7.88 to 31.52
- second_vectors: float32 [12, 768], P(None, 'zero'), may hold values from 31.52 to 126.08
Outputs:
- block_out: bfloat16 [160, 197, 768], P(('dp', 'zero'))
- grad_input: float32 [160, 197, 768], P(('dp', 'zero'))
- grad_qkv: float32 [768, 2304], P('zero')
- grad_proj: float32 [768, 768], P('zero')
- grad_fc1: float32 [768, 3072], P('zero')
- grad_fc2: float32 [3072, 768], P('zero')
- grad_vectors: float32 [12, 768], P(None, 'zero')
- next_qkv: float32 [768, 2304], P('zero')
- next_proj: float32 [768, 768], P('zero')
- next_fc1: float32 [768, 3072], P('zero')
- next_fc2: float32 [3072, 768], P('zero')
- next_vectors: float32 [12, 768], P(None, 'zero')
- next_first_qkv: float32 [768, 2304], P('zero')
- next_first_proj: float32 [768, 768], P('zero')
- next_first_fc1: float32 [768, 3072], P('zero')
- next_first_fc2: float32 [3072, 768], P('zero')
- next_first_vectors: float32 [12, 768], P(None, 'zero')
- next_second_qkv: float32 [768, 2304], P('zero')
- next_second_proj: float32 [768, 768], P('zero')
- next_second_fc1: float32 [768, 3072], P('zero')
- next_second_fc2: float32 [3072, 768], P('zero')
- next_second_vectors: float32 [12, 768], P(None, 'zero')
Inputs may be any that keep to these rules, and one draw needn't show every extreme that they name: `counts`: in every draw some device has 5 live slots and some has 3.
All inputs are finite; a program needn't handle non-finite values.
Results may differ from a plain program's by a relative error of at most 0.012.
The roundings to bfloat16 on the way count: a program that leaves them out, or rounds other values in their place, can miss the bound.
Values may be sent and summed in bfloat16 or wider, within the bound.
A program may use at most 192 MiB of HBM per device.

v0:
```python
from functools import partial

import jax
import jax.numpy as jnp
from jax import lax
from jax.sharding import PartitionSpec as P

HEADS = 12
STEP = 10


LN_EPS = 1e-06
BETA_ONE = 0.9
BETA_TWO = 0.999
ADAM_EPS = 1e-08
RATE_MATRIX = 0.05
RATE_VECTOR = 0.2
DECAY_MATRIX = 0.05


def layer_stats(values):
    center = values - jnp.mean(values, -1, keepdims=True)
    inverse = lax.rsqrt(jnp.mean(center * center, -1, keepdims=True) + LN_EPS)
    return (center * inverse, inverse)


def norm_back(grad_rows, normed, inverse, gain_row):
    scaled = grad_rows * gain_row
    return inverse * (
        scaled
        - jnp.mean(scaled, -1, keepdims=True)
        - normed * jnp.mean(scaled * normed, -1, keepdims=True)
    )


def left_product(left_side, right_side):
    return lax.dot_general(
        left_side, right_side, (((0,), (0,)), ((), ())), preferred_element_type=jnp.float32
    )


def right_product(left_side, right_side):
    return lax.dot_general(
        left_side, right_side, (((1,), (1,)), ((), ())), preferred_element_type=jnp.float32
    )


def adamw(gradient, first_old, second_old, master, step_rate, decay_rate):
    first_new = BETA_ONE * first_old + (1.0 - BETA_ONE) * gradient
    second_new = BETA_TWO * second_old + (1.0 - BETA_TWO) * gradient * gradient
    first_hat = first_new / (1.0 - BETA_ONE**STEP)
    second_hat = second_new / (1.0 - BETA_TWO**STEP)
    master_new = master - step_rate * (
        first_hat / (jnp.sqrt(second_hat) + ADAM_EPS) + decay_rate * master
    )
    return (master_new, first_new, second_new)


def per_device(
    images,
    cotangent,
    counts,
    master_qkv,
    master_proj,
    master_fc1,
    master_fc2,
    master_vectors,
    first_qkv,
    first_proj,
    first_fc1,
    first_fc2,
    first_vectors,
    second_qkv,
    second_proj,
    second_fc1,
    second_fc2,
    second_vectors,
):
    w_qkv, w_proj, w_fc1, w_fc2, vector_copy = (
        lax.all_gather(master_qkv.astype(jnp.bfloat16), "zero", axis=0, tiled=True),
        lax.all_gather(master_proj.astype(jnp.bfloat16), "zero", axis=0, tiled=True),
        lax.all_gather(master_fc1.astype(jnp.bfloat16), "zero", axis=0, tiled=True),
        lax.all_gather(master_fc2.astype(jnp.bfloat16), "zero", axis=0, tiled=True),
        lax.all_gather(master_vectors.astype(jnp.bfloat16), "zero", axis=1, tiled=True),
    )
    vectors = vector_copy.astype(jnp.float32)
    slot_count, length, feature_width = images.shape
    row_count = slot_count * length
    head_count = HEADS
    head_width = feature_width // head_count
    score_scale = head_width ** (-0.5)
    head_shape = (slot_count, length, head_count, head_width)
    slot_live = (lax.iota(jnp.int32, slot_count) < counts[0]).astype(jnp.float32)
    row_live = jnp.repeat(slot_live, length)[:, None]
    inputs = images.astype(jnp.float32).reshape(row_count, feature_width)
    normed_one, inverse_one = layer_stats(inputs)
    hidden_one = (normed_one * vectors[0] + vectors[1]).astype(jnp.bfloat16)
    joined = jnp.dot(hidden_one, w_qkv, preferred_element_type=jnp.float32)
    queries = (joined[:, :feature_width] + vectors[2]).astype(jnp.bfloat16).reshape(head_shape)
    keys_all = joined[:, feature_width : 2 * feature_width].astype(jnp.bfloat16).reshape(head_shape)
    values_all = (
        (joined[:, 2 * feature_width :] + vectors[3]).astype(jnp.bfloat16).reshape(head_shape)
    )
    scores = (
        jnp.einsum("bqhd,bkhd->bhqk", queries, keys_all, preferred_element_type=jnp.float32)
        * score_scale
    )
    highest = jnp.max(scores, -1, keepdims=True)
    exponent = jnp.exp(scores - highest)
    totals = jnp.sum(exponent, -1, keepdims=True)
    log_total = highest + jnp.log(totals)
    probs_low = (exponent / totals).astype(jnp.bfloat16)
    attn_low = jnp.einsum(
        "bhqk,bkhd->bqhd", probs_low, values_all, preferred_element_type=jnp.float32
    )
    attn_low = attn_low.reshape(row_count, feature_width).astype(jnp.bfloat16)
    mixed_rows = inputs + jnp.dot(attn_low, w_proj, preferred_element_type=jnp.float32) + vectors[4]
    normed_two, inverse_two = layer_stats(mixed_rows)
    hidden_two = (normed_two * vectors[5] + vectors[6]).astype(jnp.bfloat16)
    fc1_bias = vectors[8:].reshape(-1)
    pre_act = jnp.dot(hidden_two, w_fc1, preferred_element_type=jnp.float32) + fc1_bias
    act_value, gelu_back = jax.vjp(partial(jax.nn.gelu, approximate=False), pre_act)
    act_low = act_value.astype(jnp.bfloat16)
    block_rows = (
        mixed_rows + jnp.dot(act_low, w_fc2, preferred_element_type=jnp.float32) + vectors[7]
    )
    block_out = (
        (block_rows * row_live).astype(jnp.bfloat16).reshape(slot_count, length, feature_width)
    )
    grad_rows = cotangent.astype(jnp.float32).reshape(row_count, feature_width) * row_live
    grad_low = grad_rows.astype(jnp.bfloat16)
    grad_fc2 = left_product(act_low, grad_low)
    bias_fc2 = jnp.sum(grad_low.astype(jnp.float32), 0)
    grad_pre = gelu_back(right_product(grad_low, w_fc2))[0]
    pre_low = grad_pre.astype(jnp.bfloat16)
    grad_fc1 = left_product(hidden_two, pre_low)
    bias_fc1 = jnp.sum(pre_low.astype(jnp.float32), 0)
    back_two = right_product(pre_low, w_fc1)
    gain_two = jnp.sum(back_two * normed_two, 0)
    shift_two = jnp.sum(back_two, 0)
    grad_mixed = grad_rows + norm_back(back_two, normed_two, inverse_two, vectors[5])
    mixed_low = grad_mixed.astype(jnp.bfloat16)
    grad_proj = left_product(attn_low, mixed_low)
    bias_proj = jnp.sum(mixed_low.astype(jnp.float32), 0)
    back_attn = right_product(mixed_low, w_proj).astype(jnp.bfloat16).reshape(head_shape)
    scores_again = (
        jnp.einsum("bqhd,bkhd->bhqk", queries, keys_all, preferred_element_type=jnp.float32)
        * score_scale
    )
    probs_again = jnp.exp(scores_again - log_total)
    grad_values = jnp.einsum(
        "bhqk,bqhd->bkhd",
        probs_again.astype(jnp.bfloat16),
        back_attn,
        preferred_element_type=jnp.float32,
    )
    grad_probs = jnp.einsum(
        "bqhd,bkhd->bhqk", back_attn, values_all, preferred_element_type=jnp.float32
    )
    grad_scores = probs_again * (grad_probs - jnp.sum(probs_again * grad_probs, -1, keepdims=True))
    scores_low = grad_scores.astype(jnp.bfloat16)
    grad_queries = (
        jnp.einsum("bhqk,bkhd->bqhd", scores_low, keys_all, preferred_element_type=jnp.float32)
        * score_scale
    )
    grad_keys = (
        jnp.einsum("bhqk,bqhd->bkhd", scores_low, queries, preferred_element_type=jnp.float32)
        * score_scale
    )
    grad_joined = jnp.concatenate(
        [
            grad_queries.reshape(row_count, feature_width),
            grad_keys.reshape(row_count, feature_width),
            grad_values.reshape(row_count, feature_width),
        ],
        1,
    ).astype(jnp.bfloat16)
    grad_qkv = left_product(hidden_one, grad_joined)
    bias_query = jnp.sum(grad_joined[:, :feature_width].astype(jnp.float32), 0)
    bias_value = jnp.sum(grad_joined[:, 2 * feature_width :].astype(jnp.float32), 0)
    back_one = right_product(grad_joined, w_qkv)
    gain_one = jnp.sum(back_one * normed_one, 0)
    shift_one = jnp.sum(back_one, 0)
    grad_input = (grad_mixed + norm_back(back_one, normed_one, inverse_one, vectors[0])).reshape(
        slot_count, length, feature_width
    )
    grad_vectors = jnp.concatenate(
        [
            jnp.stack(
                [
                    gain_one,
                    shift_one,
                    bias_query,
                    bias_value,
                    bias_proj,
                    gain_two,
                    shift_two,
                    bias_fc2,
                ]
            ),
            bias_fc1.reshape(-1, feature_width),
        ],
        0,
    )
    shard_qkv, shard_proj, shard_fc1, shard_fc2, shard_vectors = (
        lax.psum_scatter(grad_qkv, "zero", scatter_dimension=0, tiled=True),
        lax.psum_scatter(grad_proj, "zero", scatter_dimension=0, tiled=True),
        lax.psum_scatter(grad_fc1, "zero", scatter_dimension=0, tiled=True),
        lax.psum_scatter(grad_fc2, "zero", scatter_dimension=0, tiled=True),
        lax.psum_scatter(grad_vectors, "zero", scatter_dimension=1, tiled=True),
    )
    sum_qkv, sum_proj, sum_fc1, sum_fc2, sum_vectors = lax.psum(
        (shard_qkv, shard_proj, shard_fc1, shard_fc2, shard_vectors), "dp"
    )
    new_qkv = adamw(sum_qkv, first_qkv, second_qkv, master_qkv, RATE_MATRIX, DECAY_MATRIX)
    new_proj = adamw(sum_proj, first_proj, second_proj, master_proj, RATE_MATRIX, DECAY_MATRIX)
    new_fc1 = adamw(sum_fc1, first_fc1, second_fc1, master_fc1, RATE_MATRIX, DECAY_MATRIX)
    new_fc2 = adamw(sum_fc2, first_fc2, second_fc2, master_fc2, RATE_MATRIX, DECAY_MATRIX)
    new_vectors = adamw(
        sum_vectors, first_vectors, second_vectors, master_vectors, RATE_VECTOR, 0.0
    )
    return (
        block_out,
        grad_input,
        sum_qkv,
        sum_proj,
        sum_fc1,
        sum_fc2,
        sum_vectors,
        new_qkv[0],
        new_proj[0],
        new_fc1[0],
        new_fc2[0],
        new_vectors[0],
        new_qkv[1],
        new_proj[1],
        new_fc1[1],
        new_fc2[1],
        new_vectors[1],
        new_qkv[2],
        new_proj[2],
        new_fc1[2],
        new_fc2[2],
        new_vectors[2],
    )


def solution(mesh):
    placed = (
        P(("dp", "zero"), None, None),
        P(("dp", "zero"), None, None),
        P(("dp", "zero")),
        P("zero", None),
        P("zero", None),
        P("zero", None),
        P("zero", None),
        P(None, "zero"),
        P("zero", None),
        P("zero", None),
        P("zero", None),
        P("zero", None),
        P(None, "zero"),
        P("zero", None),
        P("zero", None),
        P("zero", None),
        P("zero", None),
        P(None, "zero"),
    )
    return jax.shard_map(
        per_device,
        mesh=mesh,
        in_specs=placed,
        out_specs=(
            P(("dp", "zero"), None, None),
            P(("dp", "zero"), None, None),
            P("zero", None),
            P("zero", None),
            P("zero", None),
            P("zero", None),
            P(None, "zero"),
            P("zero", None),
            P("zero", None),
            P("zero", None),
            P("zero", None),
            P(None, "zero"),
            P("zero", None),
            P("zero", None),
            P("zero", None),
            P("zero", None),
            P(None, "zero"),
            P("zero", None),
            P("zero", None),
            P("zero", None),
            P("zero", None),
            P(None, "zero"),
        ),
        check_vma=False,
    )
```

profile of v0, /device:TPU:0, one launch (start us, length us, event | category | flops | bytes accessed | tf_op | source)
XLA Modules:
  0.0 704.9 jit_solution(15431947289263217897)
XLA Ops:
  15.4 10.5 %all-gather = bf16[8,96,12]{1,2,0:T(8,128)(2,1)S(1)} all-gather(bf16[1,96,12]{1,2,0:T(8,128)(2,1)S(1)} %convert_bitcast_fusion.2), channel_id=1, replica_groups=mesh['dp'=4,'zero'=8] {'zero'}, dimensions={0}, use_global_device_ids=true | all-gather | bytes 20736 | tf_op jit(solution)/shard_map/all_gather | solution.py:84
  30.2 3.4 reshape.168
  33.7 13.5 %all-gather.6.cloned.1.call-done = bf16[768,2304]{1,0:T(8,128)(2,1)} async-done(((bf16[96,2304]{1,0:T(8,128)(2,1)}), bf16[768,2304]{1,0:T(8,128)(2,1)}) %all-gather.6.cloned.1.call-update) | async-done | bytes 3538960 | tf_op jit(solution)/shard_map/all_gather | solution.py:80
  47.2 6.0 fusion.32
  55.1 5.9 reshape.181
  61.0 6.1 copy.98
  67.0 4.3 reshape.182
  71.3 5.0 copy.99
  76.3 4.3 reshape.180
  80.7 6.2 copy.100
  86.8 3.4 multiply_reduce_fusion.1
  90.3 3.1 fusion.6
  95.0 3.4 convert_bitcast_fusion.1
  99.9 3.5 convert_element_type.106
  103.4 4.3 fusion.41
  108.3 6.9 all-gather.10.cloned.1.call-done
  115.2 34.9 %multiply_convert_fusion.1 = (bf16[985,3072]{1,0:T(8,128)(2,1)}, f32[985,3072]{1,0:T(8,128)}, f32[985,3072]{1,0:T(8,128)}) fusion(f32[3072]{0:T(1024)S(1)} %add.220, bf16[768,3072]{1,0:T(8,128)(2,1)} %all-gather.10.cloned.1.call-done, f32[985,768]{1,0:T(8,128)S(1)} %get-tuple-element.66, f32[768]{0:T(1024)S(1)} %get-tuple-element.31, ...), kind=kOutput, calls=%fused_computation.9 | convolution fusion | flops 4851306496 | bytes 38030024 | tf_op jit(solution)/shard_map/dot_general | solution.py:121
  150.0 6.4 all-gather.12.cloned.1.call-done
  156.4 18.6 %convert_reduce_fusion = (f32[3072]{0:T(1024)S(1)}, bf16[985,3072]{1,0:T(8,128)(2,1)}) fusion(f32[985,3072]{1,0:T(8,128)} %get-tuple-element.60, bf16[3072,768]{1,0:T(8,128)(2,1)} %all-gather.12.cloned.1.call-done, f32[985,768]{1,0:T(8,128)} %reshape.168, f32[985]{0:T(1024)S(1)} %mul.355, f32[985,3072]{1,0:T(8,128)} %get-tuple-element.67, f32[3072]{0:T(1024)S(1)} %add.220), kind=kOutput, calls=%fused_computation.7 | convolution fusion | flops 4700763648 | bytes 38032228 | tf_op jit(solution)/shard_map/dot_general | solution.py:43
  175.0 9.5 %multiply_reduce_fusion.3 = (f32[768]{0:T(1024)S(1)}, f32[985]{0:T(1024)S(1)}, f32[985]{0:T(1024)S(1)}, f32[768]{0:T(1024)S(1)}, f32[985,768]{1,0:T(8,128)S(1)}) fusion(f32[985,768]{1,0:T(8,128)S(1)} %get-tuple-element.66, f32[985]{0:T(1024)S(1)} %add_rsqrt_fusion.1, f32[985]{0:T(1024)S(1)} %broadcast_multiply_fusion.5, f32[768]{0:T(1024)S(1)} %get-tuple-element.32, ...), kind=kOutput, calls=%fused_computation.42 | convolution fusion | flops 4654619648 | bytes 16847248 | tf_op jit(solution)/shard_map/dot_general | solution.py:43
  190.2 4.7 convolution_convert_fusion
  194.9 5.8 reshape.183
  200.7 6.0 copy.104
  206.7 8.9 %convert_bitcast_fusion = bf16[5,197,12,64]{1,3,2,0:T(8,128)(2,1)} fusion(bf16[5,197,12,64]{1,3,2,0:T(8,128)(2,1)} %copy.104, f32[5,12,197,197]{2,3,1,0:T(8,128)} %copy-done, f32[5,12,197]{2,1,0:T(8,128)S(1)} %log_add_fusion), kind=kOutput, calls=%fused_computation.59 | convolution fusion | flops 305795232 | bytes 12387360 | tf_op jit(solution)/shard_map/bhqk,bqhd->bkhd/dot_general | solution.py:151
  215.7 8.9 %multiply_reduce_fusion = (f32[5,12,197]{2,1,0:T(8,128)S(1)}, f32[5,12,197,197]{2,3,1,0:T(8,128)}) fusion(f32[5,12,197,197]{2,3,1,0:T(8,128)} %copy-done, f32[5,12,197]{2,1,0:T(8,128)S(1)} %log_add_fusion, bf16[5,197,12,64]{1,3,2,0:T(8,128)(2,1)S(1)} %copy-done.4, bf16[5,197,12,64]{1,3,2,0:T(8,128)(2,1)S(1)} %copy-done.14), kind=kOutput, calls=%fused_computation.2 | convolution fusion | flops 307355456 | bytes 21748800 | tf_op jit(solution)/shard_map/bqhd,bkhd->bhqk/dot_general | solution.py:157
  224.7 4.6 copy.114
  229.3 6.0 reshape.172
  235.3 9.9 %multiply_convert_fusion = bf16[5,12,197,197]{2,3,1,0:T(8,128)(2,1)S(1)} fusion(f32[5,12,197,197]{2,3,1,0:T(8,128)} %get-tuple-element.70, f32[5,12,197,197]{2,3,1,0:T(8,128)} %copy-done, f32[5,12,197]{2,1,0:T(8,128)S(1)} %get-tuple-element.69, f32[5,12,197]{2,1,0:T(8,128)S(1)} %log_add_fusion), kind=kLoop, calls=%fused_computation.1 | loop fusion | flops 11642700 | bytes 23379960 | tf_op jit(solution)/shard_map/convert_element_type | solution.py:161
  247.8 3.1 copy.108
  250.9 5.5 reshape.170
  256.4 5.4 fusion.18
  261.8 3.1 copy.111
  265.0 5.6 reshape.171
  275.3 6.8 fusion.31
  282.2 11.0 %fusion.33 = f32[768,3072]{1,0:T(8,128)} fusion(bf16[985,3072]{1,0:T(8,128)(2,1)} %get-tuple-element.73, f32[985,768]{1,0:T(8,128)S(1)} %get-tuple-element.66, f32[768]{0:T(1024)S(1)} %get-tuple-element.31, f32[768]{0:T(1024)S(1)} %get-tuple-element.32, f32[985]{0:T(1024)S(1)} %add_rsqrt_fusion.1, f32[985]{0:T(1024)S(1)} %broadcast_multiply_fusion.5), kind=kOutput, calls=%fused_computation.117 | convolution fusion | flops 4651595776 | bytes 18528968 | tf_op jit(solution)/shard_map/dot_general | solution.py:37
  293.3 11.4 %fusion.29 = f32[3072,768]{1,0:T(8,128)} fusion(bf16[985,3072]{1,0:T(8,128)(2,1)} %get-tuple-element.59, f32[985,768]{1,0:T(8,128)} %reshape.168, f32[985]{0:T(1024)S(1)} %mul.355), kind=kOutput, calls=%fused_computation.113 | convolution fusion | flops 4649326080 | bytes 18518884 | tf_op jit(solution)/shard_map/dot_general | solution.py:37
  311.0 9.8 %multiply_reduce_fusion.4 = (f32[768]{0:T(1024)S(1)}, f32[985]{0:T(1024)S(1)}, f32[985]{0:T(1024)S(1)}, f32[768]{0:T(1024)S(1)}, f32[985,768]{1,0:T(8,128)}) fusion(f32[985,768]{1,0:T(8,128)S(1)} %copy-done.11, f32[985]{0:T(1024)S(1)} %copy-done.43, f32[985]{0:T(1024)S(1)} %copy-done.41, f32[768]{0:T(1024)S(1)} %copy-done.39, ...), kind=kOutput, calls=%fused_computation.44 | convolution fusion | flops 3492664576 | bytes 14154640 | tf_op jit(solution)/shard_map/dot_general | solution.py:43
  322.2 25.8 %reduce-scatter.8.cloned.1.call-done = f32[96,2304]{1,0:T(8,128)} async-done(((f32[768,2304]{1,0:T(8,128)}), f32[96,2304]{1,0:T(8,128)}) %reduce-scatter.8.cloned.1.call-update) | async-done | bytes 884752 | tf_op jit(solution)/shard_map/reduce_scatter | solution.py:206
  348.0 80.0 %reduce-scatter.12.cloned.1.call-done = f32[96,3072]{1,0:T(8,128)} async-done(((f32[768,3072]{1,0:T(8,128)}), f32[96,3072]{1,0:T(8,128)}) %reduce-scatter.12.cloned.1.call-update) | async-done | bytes 1179664 | tf_op jit(solution)/shard_map/reduce_scatter | solution.py:208
  428.0 80.0 %reduce-scatter.14.cloned.1.call-done = f32[384,768]{1,0:T(8,128)} async-done(((f32[3072,768]{1,0:T(8,128)}), f32[384,768]{1,0:T(8,128)}) %reduce-scatter.14.cloned.1.call-update) | async-done | bytes 1179664 | tf_op jit(solution)/shard_map/reduce_scatter | solution.py:209
  508.0 10.1 %multiply_convert_fusion.5 = bf16[985,768]{1,0:T(8,128)(2,1)} fusion(f32[985,768]{1,0:T(8,128)S(1)} %get-tuple-element.66, bf16[985,3072]{1,0:T(8,128)(2,1)} %get-tuple-element.59, bf16[3072,768]{1,0:T(8,128)(2,1)} %all-gather.12.cloned.1.call-done, f32[985]{0:T(1024)S(1)} %mul.355, f32[768]{0:T(1024)S(1)} %copy-done.44), kind=kOutput, calls=%fused_computation.49 | convolution fusion | flops 4650840064 | bytes 15316324 | tf_op jit(solution)/shard_map/dot_general | solution.py:125
  518.1 3.1 reshape.167
  521.3 4.5 multiply_add_fusion
  525.8 4.0 reshape.173
  529.8 15.6 %reduce-scatter.16.cloned.1.call-done = f32[96,12]{1,0:T(8,128)} async-done(((f32[768,12]{1,0:T(8,128)}), f32[96,12]{1,0:T(8,128)}) %reduce-scatter.16.cloned.1.call-update) | async-done | bytes 4624
  546.9 12.1 %psum.39 = f32[12,96]{1,0:T(8,128)S(1)} all-reduce(f32[12,96]{1,0:T(8,128)} %copy.120), channel_id=1, replica_groups=mesh['dp'=4,'zero'=8] {'dp'}, use_global_device_ids=true, to_apply=%region_29.0 | all-reduce | flops 1152 | bytes 9216 | tf_op jit(solution)/shard_map/psum | solution.py:212
  560.4 122.5 %all-reduce.3.cloned.1.call-done = (f32[96,2304]{1,0:T(8,128)}, f32[96,768]{1,0:T(8,128)}, f32[96,3072]{1,0:T(8,128)}, f32[384,768]{1,0:T(8,128)}) async-done(((f32[96,2304]{1,0:T(8,128)}, f32[96,768]{1,0:T(8,128)}, f32[96,3072]{1,0:T(8,128)}, f32[384,768]{1,0:T(8,128)}), (f32[96,2304]{1,0:T(8,128)}, f32[96,768]{1,0:T(8,128)}, f32[96,3072]{1,0:T(8,128)}, f32[384,768]{1,0:T(8,128)})) %all-reduce.3.cloned.1.call-update) | async-done | bytes 3538960 | tf_op jit(solution)/shard_map/psum | solution.py:212
  685.0 3.2 multiply_subtract_fusion.2
  (179 shorter events, 52.3 us)
Async XLA Ops:
  7.2 4.0 copy-start.16
  7.2 40.0 %all-gather.6.cloned.1.call-start = ((), (), s32[]{:S(2)}) async-start(), calls=%async_computation.5 | async-start | bytes 3981312 | tf_op jit(solution)/shard_map/all_gather | solution.py:80
  9.3 5.1 copy-start.6
  9.3 94.1 %all-gather.8.cloned.1.call-start = ((), (), s32[]{:S(2)}) async-start(), calls=%async_computation.6 | async-start | bytes 1327104 | tf_op jit(solution)/shard_map/all_gather | solution.py:81
  11.2 104.0 %all-gather.10.cloned.1.call-start = ((), (), s32[]{:S(2)}) async-start(), calls=%async_computation.7 | async-start | bytes 5308416 | tf_op jit(solution)/shard_map/all_gather | solution.py:82
  12.1 3.3 copy-start.35
  12.1 144.3 %all-gather.12.cloned.1.call-start = ((), (), s32[]{:S(2)}) async-start(), calls=%async_computation.8 | async-start | bytes 5308416 | tf_op jit(solution)/shard_map/all_gather | solution.py:83
  14.3 307.8 %reduce-scatter.10.cloned.1.call-start = ((), (), s32[]{:S(2)}) async-start(), calls=%async_computation.10 | async-start | bytes 2654208 | tf_op jit(solution)/shard_map/reduce_scatter | solution.py:207
  14.8 32.4 %copy-start.40 = (f32[985]{0:T(1024)}, f32[985]{0:T(1024)S(1)}, u32[]{:S(2)}) copy-start(f32[985]{0:T(1024)S(1)} %div.110) | copy-start | bytes 11824
  26.7 20.5 %copy-start.38 = (f32[768]{0:T(1024)}, f32[768]{0:T(1024)S(1)}, u32[]{:S(2)}) copy-start(f32[768]{0:T(1024)S(1)} %get-tuple-element.37) | copy-start | bytes 9220
  26.7 20.5 %copy-start.45 = (f32[768]{0:T(1024)}, f32[768]{0:T(1024)S(1)}, u32[]{:S(2)}) copy-start(f32[768]{0:T(1024)S(1)} %get-tuple-element.36) | copy-start | bytes 9220
  28.7 18.5 %copy-start.9 = (f32[985,768]{1,0:T(8,128)S(1)}, f32[985,768]{1,0:T(8,128)}, u32[]{:S(2)}) copy-start(f32[985,768]{1,0:T(8,128)} %reshape.163) | copy-start | bytes 9077764
  30.2 23.0 %copy-start.42 = (f32[985]{0:T(1024)}, f32[985]{0:T(1024)S(1)}, u32[]{:S(2)}) copy-start(f32[985]{0:T(1024)S(1)} %rsqrt.20) | copy-start | bytes 11824
  76.3 10.5 %copy-start.2 = (bf16[5,197,12,64]{1,3,2,0:T(8,128)(2,1)}, bf16[5,197,12,64]{1,3,2,0:T(8,128)(2,1)S(1)}, u32[]{:S(2)}) copy-start(bf16[5,197,12,64]{1,3,2,0:T(8,128)(2,1)S(1)} %copy.99) | copy-start | bytes 4538884
  90.2 4.8 copy-start
  90.2 4.8 copy-start.13
  175.0 9.5 %copy-start.12 = (f32[985,768]{1,0:T(8,128)S(1)}, f32[985,768]{1,0:T(8,128)}, u32[]{:S(2)}) copy-start(f32[985,768]{1,0:T(8,128)} %reshape.168) | copy-start | bytes 9077764
  184.5 2.9 copy-start.23
  206.7 8.9 %copy-start.4 = (bf16[5,197,12,64]{1,3,2,0:T(8,128)(2,1)S(1)}, bf16[5,197,12,64]{1,3,2,0:T(8,128)(2,1)}, u32[]{:S(2)}) copy-start(bf16[5,197,12,64]{1,3,2,0:T(8,128)(2,1)} %copy.104) | copy-start | bytes 4538884
  206.7 8.9 %copy-start.14 = (bf16[5,197,12,64]{1,3,2,0:T(8,128)(2,1)S(1)}, bf16[5,197,12,64]{1,3,2,0:T(8,128)(2,1)}, u32[]{:S(2)}) copy-start(bf16[5,197,12,64]{1,3,2,0:T(8,128)(2,1)} %copy.100) | copy-start | bytes 4538884
  224.6 123.3 %reduce-scatter.8.cloned.1.call-start = ((), (), s32[]{:S(2)}) async-start(), calls=%async_computation.9 | async-start | bytes 7962624 | tf_op jit(solution)/shard_map/reduce_scatter | solution.py:206
  235.3 9.9 %copy-start.3 = (bf16[5,197,12,64]{1,3,2,0:T(8,128)(2,1)S(1)}, bf16[5,197,12,64]{1,3,2,0:T(8,128)(2,1)}, u32[]{:S(2)}) copy-start(bf16[5,197,12,64]{1,3,2,0:T(8,128)(2,1)} %copy-done.2) | copy-start | bytes 4538884
  272.4 2.9 copy-start.39
  272.4 2.9 copy-start.41
  272.4 2.9 copy-start.43
  272.4 2.9 copy-start.46
  282.1 145.8 %reduce-scatter.12.cloned.1.call-start = ((), (), s32[]{:S(2)}) async-start(), calls=%async_computation.11 | async-start | bytes 10616832 | tf_op jit(solution)/shard_map/reduce_scatter | solution.py:208
  293.2 214.8 %reduce-scatter.14.cloned.1.call-start = ((), (), s32[]{:S(2)}) async-start(), calls=%async_computation.12 | async-start | bytes 10616832 | tf_op jit(solution)/shard_map/reduce_scatter | solution.py:209
  304.7 240.7 %reduce-scatter.16.cloned.1.call-start = ((), (), s32[]{:S(2)}) async-start(), calls=%async_computation.13 | async-start | bytes 442368
  307.4 3.7 copy-start.11
  320.9 187.1 %copy-start.44 = (f32[768]{0:T(1024)S(1)}, f32[768]{0:T(1024)}, u32[]{:S(2)}) copy-start(f32[768]{0:T(1024)} %get-tuple-element.30) | copy-start | bytes 9220
  321.9 361.0 %all-reduce.3.cloned.1.call-start = ((), (), s32[]{:S(2)}) async-start(), calls=%async_computation.14 | async-start | bytes 7077888 | tf_op jit(solution)/shard_map/psum | solution.py:212
  518.1 3.1 copy-start.8
  525.7 33.3 %copy-start.36 = (f32[12,96]{1,0:T(8,128)S(1)}, f32[12,96]{1,0:T(8,128)}, u32[]{:S(2)}) copy-start(f32[12,96]{1,0:T(8,128)} %param.25) | copy-start | bytes 13828
  525.7 157.1 %copy-start.24 = (f32[96,768]{1,0:T(8,128)S(1)}, f32[96,768]{1,0:T(8,128)}, u32[]{:S(2)}) copy-start(f32[96,768]{1,0:T(8,128)} %param.22) | copy-start | bytes 884740
  525.7 157.1 %copy-start.33 = (f32[96,768]{1,0:T(8,128)S(1)}, f32[96,768]{1,0:T(8,128)}, u32[]{:S(2)}) copy-start(f32[96,768]{1,0:T(8,128)} %param.27) | copy-start | bytes 884740
  525.7 157.1 %copy-start.34 = (f32[96,768]{1,0:T(8,128)S(1)}, f32[96,768]{1,0:T(8,128)}, u32[]{:S(2)}) copy-start(f32[96,768]{1,0:T(8,128)} %param.32) | copy-start | bytes 884740
  525.8 159.1 %copy-start.22 = (f32[96,2304]{1,0:T(8,128)S(1)}, f32[96,2304]{1,0:T(8,128)}, u32[]{:S(2)}) copy-start(f32[96,2304]{1,0:T(8,128)} %param.21) | copy-start | bytes 2654212
  525.8 159.1 %copy-start.30 = (f32[96,2304]{1,0:T(8,128)S(1)}, f32[96,2304]{1,0:T(8,128)}, u32[]{:S(2)}) copy-start(f32[96,2304]{1,0:T(8,128)} %param.26) | copy-start | bytes 2654212
  525.8 159.1 %copy-start.31 = (f32[96,2304]{1,0:T(8,128)S(1)}, f32[96,2304]{1,0:T(8,128)}, u32[]{:S(2)}) copy-start(f32[96,2304]{1,0:T(8,128)} %param.31) | copy-start | bytes 2654212
  559.0 129.1 %copy-start.37 = (f32[12,96]{1,0:T(8,128)}, f32[12,96]{1,0:T(8,128)S(1)}, u32[]{:S(2)}) copy-start(f32[12,96]{1,0:T(8,128)S(1)} %psum.39) | copy-start | bytes 13828
  684.9 3.3 copy-start.17
  684.9 3.3 copy-start.20
  684.9 3.3 copy-start.26
  684.9 3.3 copy-start.27
  688.2 3.2 copy-start.28
  688.2 3.6 copy-start.29
  691.8 3.3 copy-start.25
  (11 other events, 21.9 us)
Sparse Core Ops, SparseCore 0:
  10.5 36.6 all-gather.5
  49.6 24.0 all-gather.7
  76.2 38.9 all-gather.9
  117.5 38.9 all-gather.11
  224.7 42.4 reduce-scatter.9
  282.2 65.6 reduce-scatter.7
  351.4 76.4 reduce-scatter.11
  431.5 76.4 reduce-scatter.13
  511.6 33.7 reduce-scatter.15
  547.9 134.9 all-reduce.2
where the time goes:
time: 712 us; the launch traced here: 705 us
  waiting for transfers between devices  351 us (49%)
  matrix products  161 us (23%)
  local copies, waits for them, and re-layouts  108 us (15%)
  other arithmetic  45.7 us (6%)
  blocking collectives  22.6 us (3%)
  between operations  15.8 us (2%)
    psum x1, waiting for transfers between devices, per_device(): lax.psum((shard_qkv, shard_proj, shard_fc1, shard_fc2, shard_vectors), 'dp')  122 us
    reduce_scatter x1, waiting for transfers between devices, per_device(): lax.psum_scatter(grad_fc2, 'zero', scatter_dimension=0, tiled=True)  80 us
    reduce_scatter x1, waiting for transfers between devices, per_device(): lax.psum_scatter(grad_fc1, 'zero', scatter_dimension=0, tiled=True)  80 us
    dot_general x4, matrix products, right_product(): lax.dot_general(left_side, right_side, (((1,), (1,)), ((), ())), preferre...  42.6 us
    dot_general x1, matrix products, per_device(): jnp.dot(hidden_two, w_fc1, preferred_element_type=jnp.float32) + fc1_bias  34.9 us
    dot_general x4, matrix products, left_product(): lax.dot_general(left_side, right_side, (((0,), (0,)), ((), ())), preferre...  32.1 us
    reduce_scatter x1, waiting for transfers between devices, per_device(): lax.psum_scatter(grad_qkv, 'zero', scatter_dimension=0, tiled=True)  25.8 us
    unnamed x106, local copies, waits for them, and re-layouts  17.6 us
  transfers between devices with their start and end apart: 10, of which 8 were waited for; matrix products, arithmetic and copies ran while one was open for 32% of the time, Pallas kernels for 0%

commit v1 on v0

v1 whole, which is shorter than its diff:
```python
from functools import partial

import jax
import jax.numpy as jnp
from jax import lax
from jax.experimental import pallas as pl
from jax.experimental.pallas import tpu as pltpu
from jax.sharding import PartitionSpec as P

HEADS = 12
STEP = 10


LN_EPS = 1e-06
BETA_ONE = 0.9
BETA_TWO = 0.999
ADAM_EPS = 1e-08
RATE_MATRIX = 0.05
RATE_VECTOR = 0.2
DECAY_MATRIX = 0.05


def layer_stats(values):
    center = values - jnp.mean(values, -1, keepdims=True)
    inverse = lax.rsqrt(jnp.mean(center * center, -1, keepdims=True) + LN_EPS)
    return (center * inverse, inverse)


def norm_back(grad_rows, normed, inverse, gain_row):
    scaled = grad_rows * gain_row
    return inverse * (
        scaled
        - jnp.mean(scaled, -1, keepdims=True)
        - normed * jnp.mean(scaled * normed, -1, keepdims=True)
    )


def left_product(left_side, right_side):
    return lax.dot_general(
        left_side, right_side, (((0,), (0,)), ((), ())), preferred_element_type=jnp.float32
    )


def right_product(left_side, right_side):
    return lax.dot_general(
        left_side, right_side, (((1,), (1,)), ((), ())), preferred_element_type=jnp.float32
    )


def adamw(gradient, first_old, second_old, master, step_rate, decay_rate):
    first_new = BETA_ONE * first_old + (1.0 - BETA_ONE) * gradient
    second_new = BETA_TWO * second_old + (1.0 - BETA_TWO) * gradient * gradient
    first_hat = first_new / (1.0 - BETA_ONE**STEP)
    second_hat = second_new / (1.0 - BETA_TWO**STEP)
    master_new = master - step_rate * (
        first_hat / (jnp.sqrt(second_hat) + ADAM_EPS) + decay_rate * master
    )
    return (master_new, first_new, second_new)


def swap(value, axis, size, bit):
    return lax.ppermute(value, axis, [(i, i ^ (1 << bit)) for i in range(size)])


def bit_orders(size):
    chip_bits = list(range(1, size.bit_length() - 1))
    half = len(chip_bits) // 2
    return chip_bits, chip_bits[half:] + chip_bits[:half]


def gather_bits(value, held_bits, order, size):
    index = lax.axis_index("zero")
    held_bits = list(held_bits)
    for bit in order:
        other = swap(value, "zero", size, bit)
        first = (index >> bit) & 1 == 0
        place = sum(1 for held in held_bits if held > bit)
        value = jnp.stack(
            [jnp.where(first, value, other), jnp.where(first, other, value)], axis=place
        )
        held_bits.append(bit)
    return value, held_bits


def gather_rows(block):
    size = lax.axis_size("zero")
    rows, columns = block.shape
    low = block.astype(jnp.bfloat16)
    order_one, order_two = bit_orders(size)
    part_one, held = gather_bits(low[: rows // 2], [], order_one[::-1], size)
    part_two, _ = gather_bits(low[rows // 2 :], [], order_two[::-1], size)
    whole = jnp.concatenate([part_one, part_two], axis=-2)
    whole, _ = gather_bits(whole, held, [0], size)
    return whole.reshape(size * rows, columns)


def halve_bits(value, held_bits, order, size):
    index = lax.axis_index("zero")
    held_bits = list(held_bits)
    for bit in order:
        place = held_bits.index(bit)
        mine = (index >> bit) & 1
        sent = lax.dynamic_index_in_dim(value, 1 - mine, place, keepdims=False)
        kept = lax.dynamic_index_in_dim(value, mine, place, keepdims=False)
        came = swap(sent, "zero", size, bit)
        value = (kept.astype(jnp.float32) + came.astype(jnp.float32)).astype(value.dtype)
        held_bits.remove(bit)
    return value, held_bits


def sum_line(value):
    count = lax.axis_size("dp")
    if count % 2 == 1:
        return lax.psum(value.astype(jnp.float32), "dp")
    index = lax.axis_index("dp")
    half = count // 2

    def add(left, right):
        return (left.astype(jnp.float32) + right.astype(jnp.float32)).astype(value.dtype)

    total = value
    for step in range(half - 1):
        pairs = [(step, step + 1), (count - 1 - step, count - 2 - step)]
        total = add(total, lax.ppermute(total, "dp", pairs))
    total = add(total, lax.ppermute(total, "dp", [(half - 1, half), (half, half - 1)]))
    for step in range(half - 2, -1, -1):
        pairs = [(step + 1, step), (count - 2 - step, count - 1 - step)]
        came = lax.ppermute(total, "dp", pairs)
        total = jnp.where((index == step) | (index == count - 1 - step), came, total)
    return total.astype(jnp.float32)


def reduce_rows(partial_sum):
    size = lax.axis_size("zero")
    rows = partial_sum.shape[0] // size
    columns = partial_sum.shape[1]
    bits = size.bit_length() - 1
    held = list(range(bits - 1, -1, -1))
    order_one, order_two = bit_orders(size)
    value = partial_sum.reshape((2,) * bits + (rows, columns))
    value, held = halve_bits(value, held, [0], size)
    part_one, _ = halve_bits(value[..., : rows // 2, :], held, order_one, size)
    part_two, _ = halve_bits(value[..., rows // 2 :, :], held, order_two, size)
    return jnp.concatenate([sum_line(part_one), sum_line(part_two)], axis=0)


def gather_vectors(block):
    size = lax.axis_size("zero")
    order_one, _ = bit_orders(size)
    whole, _ = gather_bits(block.astype(jnp.bfloat16), [], order_one[::-1] + [0], size)
    rows, columns = block.shape
    return whole.reshape(size, rows, columns).transpose(1, 0, 2).reshape(rows, size * columns)


def reduce_vectors(partial_sum):
    size = lax.axis_size("zero")
    rows, columns = partial_sum.shape
    bits = size.bit_length() - 1
    order_one, _ = bit_orders(size)
    value = partial_sum.reshape(rows, size, columns // size).transpose(1, 0, 2)
    value = value.reshape((2,) * bits + (rows, columns // size))
    value, _ = halve_bits(value, list(range(bits - 1, -1, -1)), [0] + order_one, size)
    return sum_line(value)


def contract(left_side, right_side, left_dim, right_dim):
    return lax.dot_general(
        left_side,
        right_side,
        (((left_dim,), (right_dim,)), ((), ())),
        preferred_element_type=jnp.float32,
    )


def head_masks(padded):
    lane = lax.broadcasted_iota(jnp.int32, (padded, 128), 1)
    return lane < 64, lane >= 64


def attend_kernel(length, scale, joined_ref, attn_ref, lse_ref):
    padded, width = attn_ref.shape[1:]
    masks = head_masks(padded)
    live = lax.broadcasted_iota(jnp.int32, (padded, padded), 0) < length
    zero = jnp.zeros((padded, 128), jnp.bfloat16)
    for pair in range(width // 128):
        at = pair * 128
        queries = joined_ref[0, :, at : at + 128] * jnp.bfloat16(scale)
        keys = joined_ref[0, :, width + at : width + at + 128]
        values = joined_ref[0, :, 2 * width + at : 2 * width + at + 128]
        outs = []
        for half in range(2):
            query = jnp.where(masks[half], queries, zero)
            scores = jnp.where(live, contract(keys, query, 1, 1), -1e30)
            highest = jnp.max(scores, 0, keepdims=True)
            exponent = jnp.exp(scores - highest)
            total = jnp.sum(exponent, 0, keepdims=True)
            head = 2 * pair + half
            lse_ref[0, head : head + 1, :] = highest + jnp.log(total)
            probs = (exponent * (1.0 / total)).astype(jnp.bfloat16)
            outs.append(contract(probs, values, 0, 0))
        attn_ref[0, :, at : at + 128] = jnp.where(masks[0], outs[0], outs[1]).astype(jnp.bfloat16)


def attend_back_kernel(length, scale, joined_ref, lse_ref, back_ref, out_ref):
    padded, width = back_ref.shape[1:]
    masks = head_masks(padded)
    live = lax.broadcasted_iota(jnp.int32, (padded, padded), 0) < length
    zero = jnp.zeros((padded, 128), jnp.bfloat16)
    for pair in range(width // 128):
        at = pair * 128
        queries = joined_ref[0, :, at : at + 128] * jnp.bfloat16(scale)
        keys = joined_ref[0, :, width + at : width + at + 128]
        keys_scaled = keys * jnp.bfloat16(scale)
        values = joined_ref[0, :, 2 * width + at : 2 * width + at + 128]
        backs = back_ref[0, :, at : at + 128]
        grads = [0.0, 0.0, 0.0]
        for half in range(2):
            head = 2 * pair + half
            query = jnp.where(masks[half], queries, zero)
            key = jnp.where(masks[half], keys_scaled, zero)
            back = jnp.where(masks[half], backs, zero)
            scores = contract(keys, query, 1, 1)
            probs = jnp.where(live, jnp.exp(scores - lse_ref[0, head : head + 1, :]), 0.0)
            grad_probs = contract(values, back, 1, 1)
            inner = jnp.sum(probs * grad_probs, 0, keepdims=True)
            low = (probs * (grad_probs - inner)).astype(jnp.bfloat16)
            grads[0] += contract(low, key, 0, 0)
            grads[1] += contract(low, query, 1, 0)
            grads[2] += contract(probs.astype(jnp.bfloat16), back, 1, 0)
        for part in range(3):
            start = part * width + at
            out_ref[0, :, start : start + 128] = grads[part].astype(jnp.bfloat16)


def slot_block(rows, columns):
    return pl.BlockSpec((1, rows, columns), lambda slot: (slot, 0, 0))


KERNEL_PARAMS = pltpu.CompilerParams(vmem_limit_bytes=40 * 2**20)


def attend(joined, length, scale, head_rows):
    slots, padded, triple = joined.shape
    width = triple // 3
    return pl.pallas_call(
        partial(attend_kernel, length, scale),
        grid=(slots,),
        in_specs=[slot_block(padded, triple)],
        out_specs=[slot_block(padded, width), slot_block(head_rows, padded)],
        out_shape=[
            jax.ShapeDtypeStruct((slots, padded, width), jnp.bfloat16),
            jax.ShapeDtypeStruct((slots, head_rows, padded), jnp.float32),
        ],
        compiler_params=KERNEL_PARAMS,
        cost_estimate=pl.CostEstimate(
            flops=slots * 12 * padded * padded * 64 * 16,
            bytes_accessed=slots * padded * width * 8,
            transcendentals=slots * 12 * padded * padded,
        ),
        name="attend",
    )(joined)


def attend_back(joined, lse, back, length, scale):
    slots, padded, triple = joined.shape
    width = triple // 3
    return pl.pallas_call(
        partial(attend_back_kernel, length, scale),
        grid=(slots,),
        in_specs=[
            slot_block(padded, triple),
            slot_block(lse.shape[1], padded),
            slot_block(padded, width),
        ],
        out_specs=slot_block(padded, triple),
        out_shape=jax.ShapeDtypeStruct((slots, padded, triple), jnp.bfloat16),
        compiler_params=KERNEL_PARAMS,
        cost_estimate=pl.CostEstimate(
            flops=slots * 12 * padded * padded * 64 * 40,
            bytes_accessed=slots * padded * width * 14,
            transcendentals=slots * 12 * padded * padded,
        ),
        name="attend_back",
    )(joined, lse, back)


def per_device(
    images,
    cotangent,
    counts,
    master_qkv,
    master_proj,
    master_fc1,
    master_fc2,
    master_vectors,
    first_qkv,
    first_proj,
    first_fc1,
    first_fc2,
    first_vectors,
    second_qkv,
    second_proj,
    second_fc1,
    second_fc2,
    second_vectors,
):
    vectors = gather_vectors(master_vectors).astype(jnp.float32)
    w_qkv = gather_rows(master_qkv)
    w_proj = gather_rows(master_proj)
    w_fc1 = gather_rows(master_fc1)
    w_fc2 = gather_rows(master_fc2)
    slot_count, length, feature_width = images.shape
    padded = -(-length // 16) * 16
    row_count = slot_count * padded
    head_width = feature_width // HEADS
    score_scale = head_width ** (-0.5)
    slot_shape = (slot_count, padded, feature_width)
    slot_live = (lax.iota(jnp.int32, slot_count) < counts[0]).astype(jnp.float32)
    row_live = jnp.repeat(slot_live, padded)[:, None]
    more_rows = ((0, 0), (0, padded - length), (0, 0))
    inputs = (
        jnp.pad(images, more_rows).astype(jnp.float32).reshape(row_count, feature_width)
    )
    normed_one, inverse_one = layer_stats(inputs)
    hidden_one = (normed_one * vectors[0] + vectors[1]).astype(jnp.bfloat16)
    joined_bias = jnp.concatenate([vectors[2], jnp.zeros_like(vectors[2]), vectors[3]])
    joined = (
        (jnp.dot(hidden_one, w_qkv, preferred_element_type=jnp.float32) + joined_bias)
        .astype(jnp.bfloat16)
        .reshape(slot_count, padded, 3 * feature_width)
    )
    attn_slots, log_total = attend(joined, length, score_scale, 16)
    attn_low = attn_slots.reshape(row_count, feature_width)
    mixed_rows = inputs + jnp.dot(attn_low, w_proj, preferred_element_type=jnp.float32) + vectors[4]
    normed_two, inverse_two = layer_stats(mixed_rows)
    hidden_two = (normed_two * vectors[5] + vectors[6]).astype(jnp.bfloat16)
    fc1_bias = vectors[8:].reshape(-1)
    pre_act = jnp.dot(hidden_two, w_fc1, preferred_element_type=jnp.float32) + fc1_bias
    act_value, gelu_back = jax.vjp(partial(jax.nn.gelu, approximate=False), pre_act)
    act_low = act_value.astype(jnp.bfloat16)
    block_rows = (
        mixed_rows + jnp.dot(act_low, w_fc2, preferred_element_type=jnp.float32) + vectors[7]
    )
    block_out = (block_rows * row_live).astype(jnp.bfloat16).reshape(slot_shape)[:, :length]
    grad_rows = (
        jnp.pad(cotangent, more_rows).astype(jnp.float32).reshape(row_count, feature_width)
        * row_live
    )
    grad_low = grad_rows.astype(jnp.bfloat16)
    sum_fc2 = reduce_rows(left_product(act_low, grad_low).astype(jnp.bfloat16))
    bias_fc2 = jnp.sum(grad_low.astype(jnp.float32), 0)
    grad_pre = gelu_back(right_product(grad_low, w_fc2))[0]
    pre_low = grad_pre.astype(jnp.bfloat16)
    sum_fc1 = reduce_rows(left_product(hidden_two, pre_low).astype(jnp.bfloat16))
    bias_fc1 = jnp.sum(pre_low.astype(jnp.float32), 0)
    back_two = right_product(pre_low, w_fc1)
    gain_two = jnp.sum(back_two * normed_two, 0)
    shift_two = jnp.sum(back_two, 0)
    grad_mixed = grad_rows + norm_back(back_two, normed_two, inverse_two, vectors[5])
    mixed_low = grad_mixed.astype(jnp.bfloat16)
    sum_proj = reduce_rows(left_product(attn_low, mixed_low).astype(jnp.bfloat16))
    bias_proj = jnp.sum(mixed_low.astype(jnp.float32), 0)
    back_attn = right_product(mixed_low, w_proj).astype(jnp.bfloat16).reshape(slot_shape)
    grad_joined = attend_back(joined, log_total, back_attn, length, score_scale).reshape(
        row_count, 3 * feature_width
    )
    sum_qkv = reduce_rows(left_product(hidden_one, grad_joined).astype(jnp.bfloat16))
    bias_query = jnp.sum(grad_joined[:, :feature_width].astype(jnp.float32), 0)
    bias_value = jnp.sum(grad_joined[:, 2 * feature_width :].astype(jnp.float32), 0)
    back_one = right_product(grad_joined, w_qkv)
    gain_one = jnp.sum(back_one * normed_one, 0)
    shift_one = jnp.sum(back_one, 0)
    grad_input = (
        grad_mixed + norm_back(back_one, normed_one, inverse_one, vectors[0])
    ).reshape(slot_shape)[:, :length]
    grad_vectors = jnp.concatenate(
        [
            jnp.stack(
                [
                    gain_one,
                    shift_one,
                    bias_query,
                    bias_value,
                    bias_proj,
                    gain_two,
                    shift_two,
                    bias_fc2,
                ]
            ),
            bias_fc1.reshape(-1, feature_width),
        ],
        0,
    )
    sum_vectors = reduce_vectors(grad_vectors)
    new_qkv = adamw(sum_qkv, first_qkv, second_qkv, master_qkv, RATE_MATRIX, DECAY_MATRIX)
    new_proj = adamw(sum_proj, first_proj, second_proj, master_proj, RATE_MATRIX, DECAY_MATRIX)
    new_fc1 = adamw(sum_fc1, first_fc1, second_fc1, master_fc1, RATE_MATRIX, DECAY_MATRIX)
    new_fc2 = adamw(sum_fc2, first_fc2, second_fc2, master_fc2, RATE_MATRIX, DECAY_MATRIX)
    new_vectors = adamw(
        sum_vectors, first_vectors, second_vectors, master_vectors, RATE_VECTOR, 0.0
    )
    return (
        block_out,
        grad_input,
        sum_qkv,
        sum_proj,
        sum_fc1,
        sum_fc2,
        sum_vectors,
        new_qkv[0],
        new_proj[0],
        new_fc1[0],
        new_fc2[0],
        new_vectors[0],
        new_qkv[1],
        new_proj[1],
        new_fc1[1],
        new_fc2[1],
        new_vectors[1],
        new_qkv[2],
        new_proj[2],
        new_fc1[2],
        new_fc2[2],
        new_vectors[2],
    )


def solution(mesh):
    placed = (
        P(("dp", "zero"), None, None),
        P(("dp", "zero"), None, None),
        P(("dp", "zero")),
        P("zero", None),
        P("zero", None),
        P("zero", None),
        P("zero", None),
        P(None, "zero"),
        P("zero", None),
        P("zero", None),
        P("zero", None),
        P("zero", None),
        P(None, "zero"),
        P("zero", None),
        P("zero", None),
        P("zero", None),
        P("zero", None),
        P(None, "zero"),
    )
    return jax.shard_map(
        per_device,
        mesh=mesh,
        in_specs=placed,
        out_specs=(
            P(("dp", "zero"), None, None),
            P(("dp", "zero"), None, None),
            P("zero", None),
            P("zero", None),
            P("zero", None),
            P("zero", None),
            P(None, "zero"),
            P("zero", None),
            P("zero", None),
            P("zero", None),
            P("zero", None),
            P(None, "zero"),
            P("zero", None),
            P("zero", None),
            P("zero", None),
            P("zero", None),
            P(None, "zero"),
            P("zero", None),
            P("zero", None),
            P("zero", None),
            P("zero", None),
            P(None, "zero"),
        ),
        check_vma=False,
    )
```

time: 712 us -> 418 us (0.59)
  waiting for transfers between devices: 351 us -> 117 us
  local copies, waits for them, and re-layouts: 108 us -> 22.1 us
  starting transfers between devices: 0.63 us -> 77.5 us
  matrix products: 161 us -> 115 us
  Pallas kernels: 0 us -> 24 us
  blocking collectives: 22.6 us -> 0 us
  between operations: 15.8 us -> 3.79 us
    reduce_scatter x4 -> x0, waiting for transfers between devices: 186 us -> none  [the longest x1 80 us: per_device(): lax.psum_scatter(grad_fc2, 'zero', scatter_dimension=0, tiled=True)]
    psum x1 -> x0, waiting for transfers between devices: 122 us -> none  [per_device(): lax.psum((shard_qkv, shard_proj, shard_fc1, shard_fc2, shard_vectors), 'dp')]
    ppermute x0 -> x73, waiting for transfers between devices: none -> 117 us  [the longest x46 58.8 us: swap(): return lax.ppermute(value, axis, [(i, i ^ 1 << bit) for i in range(size)])]
    ppermute x0 -> x73, starting transfers between devices: none -> 77.5 us  [the longest x46 37.9 us: swap(): return lax.ppermute(value, axis, [(i, i ^ 1 << bit) for i in range(size)])]
    reshape x16 -> x0, local copies, waits for them, and re-layouts: 73.2 us -> none  [the longest x2 12 us: per_device(): (joined[:, :feature_width] + vectors[2]).astype(jnp.bfloat16)]
    dot_general x7 -> x1, matrix products: 37.4 us -> 4.35 us  [per_device(): jnp.dot(hidden_one, w_qkv, preferred_element_type=jnp.float32) + joined_bias]
    all_gather x4 -> x0, waiting for transfers between devices: 26.8 us -> none  [the longest x1 13.5 us: per_device(): lax.all_gather(master_qkv.astype(jnp.bfloat16), 'zero', axis=0, tiled=True)]
    pallas_call x0 -> x2, Pallas kernels: none -> 24 us  [the longest x1 15.9 us: attend_back(): pl.pallas_call(partial(attend_back_kernel, length, scale), grid=(slots,),...]
  transfers between devices with their start and end apart: 10 -> 73, of which waited for: 8 -> 33; matrix products, arithmetic and copies ran while one was open for 32% -> 20% of each run, Pallas kernels for 0% -> 2%
where the time goes in v1:
time: 418 us; the launch traced here: 410 us
  waiting for transfers between devices  117 us (28%)
  matrix products  115 us (28%)
  starting transfers between devices  77.5 us (19%)
  other arithmetic  51.2 us (12%)
  Pallas kernels  24 us (6%)
  local copies, waits for them, and re-layouts  22.1 us (5%)
    ppermute x46, waiting for transfers between devices, swap(): return lax.ppermute(value, axis, [(i, i ^ 1 << bit) for i in range(size)])  58.8 us
    ppermute x9, waiting for transfers between devices, sum_line(): came = lax.ppermute(total, 'dp', pairs)  41.8 us
    ppermute x46, starting transfers between devices, swap(): return lax.ppermute(value, axis, [(i, i ^ 1 << bit) for i in range(size)])  37.9 us
    dot_general x1, matrix products, per_device(): jnp.dot(hidden_two, w_fc1, preferred_element_type=jnp.float32) + fc1_bias  37 us
    dot_general x4, matrix products, right_product(): lax.dot_general(left_side, right_side, (((1,), (1,)), ((), ())), preferre...  34.7 us
    dot_general x4, matrix products, left_product(): lax.dot_general(left_side, right_side, (((0,), (0,)), ((), ())), preferre...  27 us
    ppermute x9, starting transfers between devices, sum_line(): total = add(total, lax.ppermute(total, 'dp', pairs))  21.4 us
    another operation x29, other arithmetic, gather_bits(): jnp.stack([jnp.where(first, value, other), jnp.where(first, other, value)...  18.4 us
  transfers between devices with their start and end apart: 73, of which 33 were waited for; matrix products, arithmetic and copies ran while one was open for 20% of the time, Pallas kernels for 2%

profile of v1, /device:TPU:0, one launch (start us, length us, event | category | flops | bytes accessed | tf_op | source)
XLA Modules:
  0.0 410.1 jit_solution(5946910987666183261)
XLA Ops:
  3.8 3.0 collective-permute-start.18
  11.7 2.0 collective-permute-start
  19.2 2.2 fusion.14
  24.7 2.4 convert_reduce_fusion.1
  28.1 2.0 pad_convert_fusion
  39.8 2.8 collective-permute-done.11
  46.3 4.7 %collective-permute-done.5 = bf16[48,2304]{1,0:T(8,128)(2,1)S(1)} collective-permute-done((bf16[48,2304]{1,0:T(8,128)(2,1)S(1)}, bf16[48,2304]{1,0:T(8,128)(2,1)S(1)}, u32[]{:S(2)}, u32[]{:S(2)}) %collective-permute-start.5) | collective-permute-done | bytes 221216 | tf_op jit(solution)/shard_map/ppermute | solution.py:62
  57.8 8.4 %collective-permute-done.4 = bf16[2,48,2304]{2,1,0:T(8,128)(2,1)S(1)} collective-permute-done((bf16[2,48,2304]{2,1,0:T(8,128)(2,1)S(1)}, bf16[2,48,2304]{2,1,0:T(8,128)(2,1)S(1)}, u32[]{:S(2)}, u32[]{:S(2)}) %collective-permute-start.4) | collective-permute-done | bytes 442400 | tf_op jit(solution)/shard_map/ppermute | solution.py:62
  69.8 9.0 %collective-permute-done.19 = bf16[2,192,768]{2,1,0:T(8,128)(2,1)S(1)} collective-permute-done((bf16[2,192,768]{2,1,0:T(8,128)(2,1)S(1)}, bf16[2,192,768]{2,1,0:T(8,128)(2,1)S(1)}, u32[]{:S(2)}, u32[]{:S(2)}) %collective-permute-start.19) | collective-permute-done | bytes 589856 | tf_op jit(solution)/shard_map/ppermute | solution.py:62
  79.6 11.1 %collective-permute-done.14 = bf16[2,48,3072]{2,1,0:T(8,128)(2,1)S(1)} collective-permute-done((bf16[2,48,3072]{2,1,0:T(8,128)(2,1)S(1)}, bf16[2,48,3072]{2,1,0:T(8,128)(2,1)S(1)}, u32[]{:S(2)}, u32[]{:S(2)}) %collective-permute-start.14) | collective-permute-done | bytes 589856 | tf_op jit(solution)/shard_map/ppermute | solution.py:62
  94.0 4.3 %fusion.6 = bf16[1040,2304]{1,0:T(8,128)(2,1)S(1)} fusion(bf16[1040,768]{1,0:T(8,128)(2,1)S(1)} %bitcast.309, bf16[768,2304]{1,0:T(8,128)(2,1)S(1)} %bitcast.303, f32[2304]{0:T(1024)S(1)} %pad_maximum_fusion.17), kind=kOutput, calls=%fused_computation.20 | convolution fusion | flops 3685294080 | bytes 9937920 | tf_op jit(solution)/shard_map/dot_general | solution.py:328
  98.4 8.1 %attend.1 = (bf16[5,208,768]{2,1,0:T(8,128)(2,1)S(1)}, f32[5,16,208]{2,1,0:T(8,128)S(1)}) custom-call(bf16[5,208,2304]{2,1,0:T(8,128)(2,1)S(1)} %bitcast.285), custom_call_target="tpu_custom_call" | custom-call | flops 2658140160 | bytes 6389760 | tf_op jit(solution)/shard_map/attend/pallas_call | solution.py:245
  108.7 2.7 select_bitcast_fusion.1
  111.4 2.5 pad_maximum_fusion.1
  113.9 2.5 select_bitcast_fusion.3
  116.9 37.0 %multiply_convert_fusion = (bf16[1040,3072]{1,0:T(8,128)(2,1)}, f32[1040,3072]{1,0:T(8,128)}, f32[1040,3072]{1,0:T(8,128)}) fusion(f32[3072]{0:T(1024)S(1)} %add.386, bf16[768,3072]{1,0:T(8,128)(2,1)S(1)} %bitcast.301, f32[1040,768]{1,0:T(8,128)S(1)} %get-tuple-element.150, f32[768]{0:T(1024)S(1)} %add.383, f32[768]{0:T(1024)S(1)} %mul.337, ...), kind=kOutput, calls=%fused_computation.6 | convolution fusion | flops 5122191360 | bytes 39889024 | tf_op jit(solution)/shard_map/dot_general | solution.py:338
  153.9 16.7 %convert_reduce_fusion = (f32[3072]{0:T(1024)S(1)}, bf16[1040,3072]{1,0:T(8,128)(2,1)}) fusion(f32[1040,3072]{1,0:T(8,128)} %get-tuple-element.63, f32[1040,3072]{1,0:T(8,128)} %get-tuple-element.151, bf16[1040,768]{1,0:T(8,128)(2,1)S(1)} %bitcast.308, bf16[3072,768]{1,0:T(8,128)(2,1)} %bitcast.299), kind=kOutput, calls=%fused_computation.4 | convolution fusion | flops 4958450688 | bytes 38277120 | tf_op jit(solution)/shard_map/dot_general | solution.py:45
  170.5 10.3 %multiply_reduce_fusion = (f32[768]{0:T(1024)S(1)}, f32[1040]{0:T(1024)S(1)}, f32[1040]{0:T(1024)S(1)}, f32[768]{0:T(1024)S(1)}, f32[1040,768]{1,0:T(8,128)S(1)}) fusion(f32[1040,768]{1,0:T(8,128)S(1)} %get-tuple-element.150, f32[1040]{0:T(1024)S(1)} %add_rsqrt_fusion, f32[1040]{0:T(1024)S(1)} %broadcast_multiply_fusion.4, f32[768]{0:T(1024)S(1)} %mul.337, ...), kind=kOutput, calls=%fused_computation.44 | convolution fusion | flops 4914520064 | bytes 17523968 | tf_op jit(solution)/shard_map/dot_general | solution.py:45
  180.9 9.0 %convolution_convert_fusion.1 = bf16[768,3072]{1,0:T(8,128)(2,1)} fusion(bf16[1040,3072]{1,0:T(8,128)(2,1)S(1)} %copy-done.68, f32[1040,768]{1,0:T(8,128)S(1)} %get-tuple-element.150, f32[768]{0:T(1024)S(1)} %add.383, f32[768]{0:T(1024)S(1)} %mul.337, f32[1040]{0:T(1024)S(1)} %add_rsqrt_fusion, f32[1040]{0:T(1024)S(1)} %broadcast_multiply_fusion.4), kind=kOutput, calls=%fused_computation.23 | convolution fusion | flops 4913688576 | bytes 14317696 | tf_op jit(solution)/shard_map/dot_general | solution.py:39
  194.0 2.8 convolution_convert_fusion.3
  196.8 15.9 %attend_back.1 = bf16[5,208,2304]{2,1,0:T(8,128)(2,1)S(1)} custom-call(bf16[5,208,2304]{2,1,0:T(8,128)(2,1)S(1)} %bitcast.288, f32[5,16,208]{2,1,0:T(8,128)S(1)} %get-tuple-element.25.lse_ref, bf16[5,208,768]{2,1,0:T(8,128)(2,1)S(1)} %bitcast.291), custom_call_target="tpu_custom_call" | custom-call | flops 6645350400 | bytes 11182080 | tf_op jit(solution)/shard_map/attend_back/pallas_call | solution.py:267
  212.7 6.7 %bitcast_convert_fusion = bf16[768,2304]{1,0:T(8,128)(2,1)} fusion(bf16[5,208,2304]{2,1,0:T(8,128)(2,1)S(1)} %attend_back.1, f32[768]{0:T(1024)S(1)} %copy-done.62, f32[768]{0:T(1024)S(1)} %copy-done.59, f32[5,208]{1,0:T(8,128)S(1)} %copy-done.51, f32[5,208]{1,0:T(8,128)S(1)} %copy-done.49, bf16[5,197,768]{2,1,0:T(8,128)(2,1)S(1)} %copy-done.4), kind=kOutput, calls=%fused_computation.21 | convolution fusion | flops 3687063552 | bytes 9858688 | tf_op jit(solution)/shard_map/dot_general | solution.py:39
  221.3 6.2 %fusion.40 = (f32[768]{0:T(1024)S(1)}, f32[768]{0:T(1024)S(1)}, f32[1040]{0:T(1024)S(1)}, f32[1040]{0:T(1024)S(1)}, f32[1040,768]{1,0:T(8,128)}) fusion(f32[1040]{0:T(1024)S(1)} %copy-done.57, f32[1040]{0:T(1024)S(1)} %copy-done.55, bf16[5,197,768]{2,1,0:T(8,128)(2,1)S(1)} %copy-done.4, f32[1040,768]{1,0:T(8,128)S(1)} %copy-done.23, ...), kind=kOutput, calls=%fused_computation.267 | convolution fusion | flops 3688485376 | bytes 16259840 | tf_op jit(solution)/shard_map/dot_general | solution.py:45
  228.8 8.5 %convolution_convert_fusion = bf16[3072,768]{1,0:T(8,128)(2,1)S(1)} fusion(bf16[1040,3072]{1,0:T(8,128)(2,1)} %get-tuple-element.62, bf16[1040,768]{1,0:T(8,128)(2,1)S(1)} %get-tuple-element.76), kind=kOutput, calls=%fused_computation.22 | convolution fusion | flops 4909694976 | bytes 12705792 | tf_op jit(solution)/shard_map/dot_general | solution.py:39
  237.7 2.0 dynamic-slice_bitcast_fusion.1
  244.2 10.0 %fusion.13 = bf16[1040,768]{1,0:T(8,128)(2,1)} fusion(f32[1040,768]{1,0:T(8,128)S(1)} %copy-done.6, bf16[1040,3072]{1,0:T(8,128)(2,1)} %get-tuple-element.62, bf16[3072,768]{1,0:T(8,128)(2,1)} %bitcast.300, f32[1040]{0:T(1024)S(1)} %copy-done.60, f32[768]{0:T(1024)S(1)} %copy-done.66), kind=kOutput, calls=%fused_computation.38 | convolution fusion | flops 4910530560 | bytes 15907904 | tf_op jit(solution)/shard_map/dot_general | solution.py:342
  254.9 3.1 collective-permute-done.69
  258.0 3.5 collective-permute-start.70
  271.8 4.3 %collective-permute-done.72 = f32[12,96]{1,0:T(8,128)S(1)} collective-permute-done((f32[12,96]{1,0:T(8,128)S(1)}, f32[12,96]{1,0:T(8,128)S(1)}, u32[]{:S(2)}, u32[]{:S(2)}) %collective-permute-start.72) | collective-permute-done | bytes 4640 | tf_op jit(solution)/shard_map/ppermute | solution.py:128
  279.0 3.0 collective-permute-done.40
  283.1 4.3 %collective-permute-start.37 = (bf16[48,768]{1,0:T(8,128)(2,1)S(1)}, bf16[48,768]{1,0:T(8,128)(2,1)S(1)}, u32[]{:S(2)}, u32[]{:S(2)}) collective-permute-start(bf16[48,768]{1,0:T(8,128)(2,1)S(1)} %fusion.36), channel_id=1, source_target_pairs={{0,8},{24,16},{1,9},{25,17},{2,10},{26,18},{3,11},{27,19},{4,12},{... | collective-permute-start | bytes 221192 | tf_op jit(solution)/shard_map/ppermute | solution.py:124
  294.5 7.2 %collective-permute-done.39 = bf16[48,768]{1,0:T(8,128)(2,1)S(1)} collective-permute-done((bf16[48,768]{1,0:T(8,128)(2,1)S(1)}, bf16[48,768]{1,0:T(8,128)(2,1)S(1)}, u32[]{:S(2)}, u32[]{:S(2)}) %collective-permute-start.39) | collective-permute-done | bytes 73760 | tf_op jit(solution)/shard_map/ppermute | solution.py:128
  301.7 2.4 collective-permute-done.44
  307.5 10.0 %collective-permute-done.24 = bf16[2,48,2304]{2,1,0:T(8,128)(2,1)S(1)} collective-permute-done((bf16[2,48,2304]{2,1,0:T(8,128)(2,1)S(1)}, bf16[2,48,2304]{2,1,0:T(8,128)(2,1)S(1)}, u32[]{:S(2)}, u32[]{:S(2)}) %collective-permute-start.24) | collective-permute-done | bytes 442400 | tf_op jit(solution)/shard_map/ppermute | solution.py:62
  329.4 3.4 collective-permute-done.26
  332.8 4.4 %collective-permute-start.31 = (bf16[48,2304]{1,0:T(8,128)(2,1)S(1)}, bf16[48,2304]{1,0:T(8,128)(2,1)S(1)}, u32[]{:S(2)}, u32[]{:S(2)}) collective-permute-start(bf16[48,2304]{1,0:T(8,128)(2,1)S(1)} %fusion.30), channel_id=1, source_target_pairs={{0,8},{24,16},{1,9},{25,17},{2,10},{26,18},{3,11},{27,19},{4,12},{... | collective-permute-start | bytes 663560 | tf_op jit(solution)/shard_map/ppermute | solution.py:124
  337.2 3.4 collective-permute-done.31
  350.0 13.9 %collective-permute-done.28 = bf16[48,2304]{1,0:T(8,128)(2,1)S(1)} collective-permute-done((bf16[48,2304]{1,0:T(8,128)(2,1)S(1)}, bf16[48,2304]{1,0:T(8,128)(2,1)S(1)}, u32[]{:S(2)}, u32[]{:S(2)}) %collective-permute-start.28) | collective-permute-done | bytes 221216 | tf_op jit(solution)/shard_map/ppermute | solution.py:128
  366.3 2.0 multiply_subtract_fusion.2
  368.4 2.3 collective-permute-start.59
  375.7 2.3 collective-permute-done.64
  378.8 2.4 collective-permute-done.48
  382.0 2.4 collective-permute-done.53
  391.0 6.1 %collective-permute-done.61 = bf16[192,768]{1,0:T(8,128)(2,1)S(1)} collective-permute-done((bf16[192,768]{1,0:T(8,128)(2,1)S(1)}, bf16[192,768]{1,0:T(8,128)(2,1)S(1)}, u32[]{:S(2)}, u32[]{:S(2)}) %collective-permute-start.61) | collective-permute-done | bytes 294944 | tf_op jit(solution)/shard_map/ppermute | solution.py:128
  397.1 3.1 collective-permute-done.66
  400.3 3.1 collective-permute-done.50
  403.5 2.7 multiply_subtract_fusion
  407.2 2.5 multiply_subtract_fusion.1
  (444 shorter events, 122.1 us)
Async XLA Ops:
  3.8 48.3 %collective-permute-start.18 = (bf16[192,768]{1,0:T(8,128)(2,1)}, bf16[192,768]{1,0:T(8,128)(2,1)}, u32[]{:S(2)}, u32[]{:S(2)}) collective-permute-start(bf16[192,768]{1,0:T(8,128)(2,1)} %get-tuple-element.107), channel_id=1, source_target_pairs={{0,4},{1,5},{2,6},{3,7},{4,0},{5,1},{6,2},{7,3},{8,12},{9,13},{10,... | collective-permute-start | bytes 884744 | tf_op jit(solution)/shard_map/ppermute | solution.py:62
  6.8 46.8 %collective-permute-start.20 = (bf16[192,768]{1,0:T(8,128)(2,1)}, bf16[192,768]{1,0:T(8,128)(2,1)}, u32[]{:S(2)}, u32[]{:S(2)}) collective-permute-start(bf16[192,768]{1,0:T(8,128)(2,1)} %get-tuple-element.108), channel_id=1, source_target_pairs={{0,2},{1,3},{2,0},{3,1},{4,6},{5,7},{6,4},{7,5},{8,10},{9,11},{10,... | collective-permute-start | bytes 884744 | tf_op jit(solution)/shard_map/ppermute | solution.py:62
  10.6 21.6 %collective-permute-start.10 = (bf16[48,768]{1,0:T(8,128)(2,1)}, bf16[48,768]{1,0:T(8,128)(2,1)}, u32[]{:S(2)}, u32[]{:S(2)}) collective-permute-start(bf16[48,768]{1,0:T(8,128)(2,1)} %get-tuple-element.128), channel_id=1, source_target_pairs={{0,2},{1,3},{2,0},{3,1},{4,6},{5,7},{6,4},{7,5},{8,10},{9,11},{10,... | collective-permute-start | bytes 221192 | tf_op jit(solution)/shard_map/ppermute | solution.py:62
  11.1 21.1 %collective-permute-start.8 = (bf16[48,768]{1,0:T(8,128)(2,1)}, bf16[48,768]{1,0:T(8,128)(2,1)}, u32[]{:S(2)}, u32[]{:S(2)}) collective-permute-start(bf16[48,768]{1,0:T(8,128)(2,1)} %get-tuple-element.127), channel_id=1, source_target_pairs={{0,4},{1,5},{2,6},{3,7},{4,0},{5,1},{6,2},{7,3},{8,12},{9,13},{10,... | collective-permute-start | bytes 221192 | tf_op jit(solution)/shard_map/ppermute | solution.py:62
  11.7 10.2 %collective-permute-start = (bf16[12,96]{1,0:T(8,128)(2,1)}, bf16[12,96]{1,0:T(8,128)(2,1)}, u32[]{:S(2)}, u32[]{:S(2)}) collective-permute-start(bf16[12,96]{1,0:T(8,128)(2,1)} %convert_element_type.495), channel_id=1, source_target_pairs={{0,4},{1,5},{2,6},{3,7},{4,0},{5,1},{6,2},{7,3},{8,12},{9,13},{10,... | collective-permute-start | bytes 6920 | tf_op jit(solution)/shard_map/ppermute | solution.py:62
  31.5 14.1 %collective-permute-start.3 = (bf16[48,2304]{1,0:T(8,128)(2,1)S(1)}, bf16[48,2304]{1,0:T(8,128)(2,1)}, u32[]{:S(2)}, u32[]{:S(2)}) collective-permute-start(bf16[48,2304]{1,0:T(8,128)(2,1)S(1)} %copy-done.47), channel_id=1, source_target_pairs={{0,4},{1,5},{2,6},{3,7},{4,0},{5,1},{6,2},{7,3},{8,12},{9,13},{10,... | collective-permute-start | bytes 663560 | tf_op jit(solution)/shard_map/ppermute | solution.py:62
  33.9 8.7 %collective-permute-start.11 = (bf16[2,48,768]{2,1,0:T(8,128)(2,1)}, bf16[2,48,768]{2,1,0:T(8,128)(2,1)}, u32[]{:S(2)}, u32[]{:S(2)}) collective-permute-start(bf16[2,48,768]{2,1,0:T(8,128)(2,1)} %pad_maximum_fusion.15), channel_id=1, source_target_pairs={{0,4},{1,5},{2,6},{3,7},{4,0},{5,1},{6,2},{7,3},{8,12},{9,13},{10,... | collective-permute-start | bytes 442376 | tf_op jit(solution)/shard_map/ppermute | solution.py:62
  35.5 8.5 %collective-permute-start.9 = (bf16[2,48,768]{2,1,0:T(8,128)(2,1)S(1)}, bf16[2,48,768]{2,1,0:T(8,128)(2,1)}, u32[]{:S(2)}, u32[]{:S(2)}) collective-permute-start(bf16[2,48,768]{2,1,0:T(8,128)(2,1)S(1)} %pad_maximum_fusion.14), channel_id=1, source_target_pairs={{0,2},{1,3},{2,0},{3,1},{4,6},{5,7},{6,4},{7,5},{8,10},{9,11},{10,... | collective-permute-start | bytes 442376 | tf_op jit(solution)/shard_map/ppermute | solution.py:62
  44.0 11.3 %collective-permute-start.13 = (bf16[48,3072]{1,0:T(8,128)(2,1)S(1)}, bf16[48,3072]{1,0:T(8,128)(2,1)S(1)}, u32[]{:S(2)}, u32[]{:S(2)}) collective-permute-start(bf16[48,3072]{1,0:T(8,128)(2,1)S(1)} %copy-done.45), channel_id=1, source_target_pairs={{0,4},{1,5},{2,6},{3,7},{4,0},{5,1},{6,2},{7,3},{8,12},{9,13},{10,... | collective-permute-start | bytes 884744 | tf_op jit(solution)/shard_map/ppermute | solution.py:62
  45.6 11.0 %collective-permute-start.15 = (bf16[48,3072]{1,0:T(8,128)(2,1)S(1)}, bf16[48,3072]{1,0:T(8,128)(2,1)S(1)}, u32[]{:S(2)}, u32[]{:S(2)}) collective-permute-start(bf16[48,3072]{1,0:T(8,128)(2,1)S(1)} %copy-done.44), channel_id=1, source_target_pairs={{0,2},{1,3},{2,0},{3,1},{4,6},{5,7},{6,4},{7,5},{8,10},{9,11},{10,... | collective-permute-start | bytes 884744 | tf_op jit(solution)/shard_map/ppermute | solution.py:62
  50.9 17.4 %collective-permute-start.12 = (bf16[2,2,96,768]{3,2,1,0:T(8,128)(2,1)S(1)}, bf16[2,2,96,768]{3,2,1,0:T(8,128)(2,1)S(1)}, u32[]{:S(2)}, u32[]{:S(2)}) collective-permute-start(bf16[2,2,96,768]{3,2,1,0:T(8,128)(2,1)S(1)} %maximum_maximum_fusion.3), channel_id=1, source_target_pairs={{0,1},{1,0},{2,3},{3,2},{4,5},{5,4},{6,7},{7,6},{8,9},{9,8},{10,11... | collective-permute-start | bytes 1769480 | tf_op jit(solution)/shard_map/ppermute | solution.py:62
  52.1 14.1 %collective-permute-start.4 = (bf16[2,48,2304]{2,1,0:T(8,128)(2,1)S(1)}, bf16[2,48,2304]{2,1,0:T(8,128)(2,1)S(1)}, u32[]{:S(2)}, u32[]{:S(2)}) collective-permute-start(bf16[2,48,2304]{2,1,0:T(8,128)(2,1)S(1)} %pad_maximum_fusion.11), channel_id=1, source_target_pairs={{0,2},{1,3},{2,0},{3,1},{4,6},{5,7},{6,4},{7,5},{8,10},{9,11},{10,... | collective-permute-start | bytes 1327112 | tf_op jit(solution)/shard_map/ppermute | solution.py:62
  53.5 14.0 %collective-permute-start.6 = (bf16[2,48,2304]{2,1,0:T(8,128)(2,1)S(1)}, bf16[2,48,2304]{2,1,0:T(8,128)(2,1)S(1)}, u32[]{:S(2)}, u32[]{:S(2)}) collective-permute-start(bf16[2,48,2304]{2,1,0:T(8,128)(2,1)S(1)} %pad_maximum_fusion.12), channel_id=1, source_target_pairs={{0,4},{1,5},{2,6},{3,7},{4,0},{5,1},{6,2},{7,3},{8,12},{9,13},{10,... | collective-permute-start | bytes 1327112 | tf_op jit(solution)/shard_map/ppermute | solution.py:62
  55.3 23.4 %collective-permute-start.19 = (bf16[2,192,768]{2,1,0:T(8,128)(2,1)S(1)}, bf16[2,192,768]{2,1,0:T(8,128)(2,1)S(1)}, u32[]{:S(2)}, u32[]{:S(2)}) collective-permute-start(bf16[2,192,768]{2,1,0:T(8,128)(2,1)S(1)} %pad_maximum_fusion.9), channel_id=1, source_target_pairs={{0,2},{1,3},{2,0},{3,1},{4,6},{5,7},{6,4},{7,5},{8,10},{9,11},{10,... | collective-permute-start | bytes 1769480 | tf_op jit(solution)/shard_map/ppermute | solution.py:62
  56.6 22.5 %collective-permute-start.21 = (bf16[2,192,768]{2,1,0:T(8,128)(2,1)S(1)}, bf16[2,192,768]{2,1,0:T(8,128)(2,1)S(1)}, u32[]{:S(2)}, u32[]{:S(2)}) collective-permute-start(bf16[2,192,768]{2,1,0:T(8,128)(2,1)S(1)} %pad_maximum_fusion.10), channel_id=1, source_target_pairs={{0,4},{1,5},{2,6},{3,7},{4,0},{5,1},{6,2},{7,3},{8,12},{9,13},{10,... | collective-permute-start | bytes 1769480 | tf_op jit(solution)/shard_map/ppermute | solution.py:62
  66.1 24.6 %collective-permute-start.14 = (bf16[2,48,3072]{2,1,0:T(8,128)(2,1)S(1)}, bf16[2,48,3072]{2,1,0:T(8,128)(2,1)S(1)}, u32[]{:S(2)}, u32[]{:S(2)}) collective-permute-start(bf16[2,48,3072]{2,1,0:T(8,128)(2,1)S(1)} %pad_maximum_fusion.7), channel_id=1, source_target_pairs={{0,2},{1,3},{2,0},{3,1},{4,6},{5,7},{6,4},{7,5},{8,10},{9,11},{10,... | collective-permute-start | bytes 1769480 | tf_op jit(solution)/shard_map/ppermute | solution.py:62
  67.5 23.6 %collective-permute-start.16 = (bf16[2,48,3072]{2,1,0:T(8,128)(2,1)S(1)}, bf16[2,48,3072]{2,1,0:T(8,128)(2,1)S(1)}, u32[]{:S(2)}, u32[]{:S(2)}) collective-permute-start(bf16[2,48,3072]{2,1,0:T(8,128)(2,1)S(1)} %pad_maximum_fusion.8), channel_id=1, source_target_pairs={{0,4},{1,5},{2,6},{3,7},{4,0},{5,1},{6,2},{7,3},{8,12},{9,13},{10,... | collective-permute-start | bytes 1769480 | tf_op jit(solution)/shard_map/ppermute | solution.py:62
  68.4 23.2 %collective-permute-start.7 = (bf16[2,2,96,2304]{3,2,1,0:T(8,128)(2,1)S(1)}, bf16[2,2,96,2304]{3,2,1,0:T(8,128)(2,1)S(1)}, u32[]{:S(2)}, u32[]{:S(2)}) collective-permute-start(bf16[2,2,96,2304]{3,2,1,0:T(8,128)(2,1)S(1)} %maximum_maximum_fusion.2), channel_id=1, source_target_pairs={{0,1},{1,0},{2,3},{3,2},{4,5},{5,4},{6,7},{7,6},{8,9},{9,8},{10,11... | collective-permute-start | bytes 5308424 | tf_op jit(solution)/shard_map/ppermute | solution.py:62
  79.6 29.1 %collective-permute-start.22 = (bf16[2,2,384,768]{3,2,1,0:T(8,128)(2,1)S(1)}, bf16[2,2,384,768]{3,2,1,0:T(8,128)(2,1)}, u32[]{:S(2)}, u32[]{:S(2)}) collective-permute-start(bf16[2,2,384,768]{3,2,1,0:T(8,128)(2,1)S(1)} %maximum_maximum_fusion.1), channel_id=1, source_target_pairs={{0,1},{1,0},{2,3},{3,2},{4,5},{5,4},{6,7},{7,6},{8,9},{9,8},{10,11... | collective-permute-start | bytes 7077896 | tf_op jit(solution)/shard_map/ppermute | solution.py:62
  91.5 22.5 %collective-permute-start.17 = (bf16[2,2,96,3072]{3,2,1,0:T(8,128)(2,1)S(1)}, bf16[2,2,96,3072]{3,2,1,0:T(8,128)(2,1)}, u32[]{:S(2)}, u32[]{:S(2)}) collective-permute-start(bf16[2,2,96,3072]{3,2,1,0:T(8,128)(2,1)S(1)} %maximum_maximum_fusion), channel_id=1, source_target_pairs={{0,1},{1,0},{2,3},{3,2},{4,5},{5,4},{6,7},{7,6},{8,9},{9,8},{10,11... | collective-permute-start | bytes 7077896 | tf_op jit(solution)/shard_map/ppermute | solution.py:62
  228.3 14.8 %collective-permute-start.67 = (f32[2,2,12,96]{3,1,2,0:T(2,128)S(1)}, f32[2,2,12,96]{3,1,2,0:T(2,128)S(1)}, u32[]{:S(2)}, u32[]{:S(2)}) collective-permute-start(f32[2,2,12,96]{3,1,2,0:T(2,128)S(1)} %bitcast.318), channel_id=1, source_target_pairs={{0,1},{1,0},{2,3},{3,2},{4,5},{5,4},{6,7},{7,6},{8,9},{9,8},{10,11... | collective-permute-start | bytes 55304 | tf_op jit(solution)/shard_map/ppermute | solution.py:62
  237.6 83.1 %collective-permute-start.56 = (bf16[2,2,384,768]{3,2,1,0:T(8,128)(2,1)S(1)}, bf16[2,2,384,768]{3,2,1,0:T(8,128)(2,1)S(1)}, u32[]{:S(2)}, u32[]{:S(2)}) collective-permute-start(bf16[2,2,384,768]{3,2,1,0:T(8,128)(2,1)S(1)} %dynamic-slice_bitcast_fusion), channel_id=1, source_target_pairs={{0,1},{1,0},{2,3},{3,2},{4,5},{5,4},{6,7},{7,6},{8,9},{9,8},{10,11... | collective-permute-start | bytes 7077896 | tf_op jit(solution)/shard_map/ppermute | solution.py:62
  239.7 83.6 %collective-permute-start.45 = (bf16[2,2,96,3072]{3,2,1,0:T(8,128)(2,1)S(1)}, bf16[2,2,96,3072]{3,2,1,0:T(8,128)(2,1)S(1)}, u32[]{:S(2)}, u32[]{:S(2)}) collective-permute-start(bf16[2,2,96,3072]{3,2,1,0:T(8,128)(2,1)S(1)} %dynamic-slice_bitcast_fusion.1), channel_id=1, source_target_pairs={{0,1},{1,0},{2,3},{3,2},{4,5},{5,4},{6,7},{7,6},{8,9},{9,8},{10,11... | collective-permute-start | bytes 7077896 | tf_op jit(solution)/shard_map/ppermute | solution.py:62
  241.2 28.2 %collective-permute-start.34 = (bf16[2,2,96,768]{3,2,1,0:T(8,128)(2,1)}, bf16[2,2,96,768]{3,2,1,0:T(8,128)(2,1)}, u32[]{:S(2)}, u32[]{:S(2)}) collective-permute-start(bf16[2,2,96,768]{3,2,1,0:T(8,128)(2,1)} %dynamic-slice_bitcast_fusion.7), channel_id=1, source_target_pairs={{0,1},{1,0},{2,3},{3,2},{4,5},{5,4},{6,7},{7,6},{8,9},{9,8},{10,11... | collective-permute-start | bytes 1769480 | tf_op jit(solution)/shard_map/ppermute | solution.py:62
  242.6 61.5 %collective-permute-start.23 = (bf16[2,2,96,2304]{3,2,1,0:T(8,128)(2,1)}, bf16[2,2,96,2304]{3,2,1,0:T(8,128)(2,1)S(1)}, u32[]{:S(2)}, u32[]{:S(2)}) collective-permute-start(bf16[2,2,96,2304]{3,2,1,0:T(8,128)(2,1)} %dynamic-slice_bitcast_fusion.2), channel_id=1, source_target_pairs={{0,1},{1,0},{2,3},{3,2},{4,5},{5,4},{6,7},{7,6},{8,9},{9,8},{10,11... | collective-permute-start | bytes 5308424 | tf_op jit(solution)/shard_map/ppermute | solution.py:62
  243.1 11.1 %collective-permute-start.68 = (f32[2,12,96]{2,0,1:T(2,128)S(1)}, f32[2,12,96]{2,0,1:T(2,128)S(1)}, u32[]{:S(2)}, u32[]{:S(2)}) collective-permute-start(f32[2,12,96]{2,0,1:T(2,128)S(1)} %bitcast.319), channel_id=1, source_target_pairs={{0,2},{1,3},{2,0},{3,1},{4,6},{5,7},{6,4},{7,5},{8,10},{9,11},{10,... | collective-permute-start | bytes 27656 | tf_op jit(solution)/shard_map/ppermute | solution.py:62
  291.9 9.8 %collective-permute-start.39 = (bf16[48,768]{1,0:T(8,128)(2,1)S(1)}, bf16[48,768]{1,0:T(8,128)(2,1)S(1)}, u32[]{:S(2)}, u32[]{:S(2)}) collective-permute-start(bf16[48,768]{1,0:T(8,128)(2,1)S(1)} %add_convert_fusion.17), channel_id=1, source_target_pairs={{8,0},{16,24},{9,1},{17,25},{10,2},{18,26},{11,3},{19,27},{12,4},{... | collective-permute-start | bytes 221192 | tf_op jit(solution)/shard_map/ppermute | solution.py:128
  293.2 10.9 %collective-permute-start.44 = (bf16[48,768]{1,0:T(8,128)(2,1)S(1)}, bf16[48,768]{1,0:T(8,128)(2,1)S(1)}, u32[]{:S(2)}, u32[]{:S(2)}) collective-permute-start(bf16[48,768]{1,0:T(8,128)(2,1)S(1)} %add_convert_fusion.15), channel_id=1, source_target_pairs={{8,0},{16,24},{9,1},{17,25},{10,2},{18,26},{11,3},{19,27},{12,4},{... | collective-permute-start | bytes 221192 | tf_op jit(solution)/shard_map/ppermute | solution.py:128
  304.8 12.8 %collective-permute-start.24 = (bf16[2,48,2304]{2,1,0:T(8,128)(2,1)S(1)}, bf16[2,48,2304]{2,1,0:T(8,128)(2,1)S(1)}, u32[]{:S(2)}, u32[]{:S(2)}) collective-permute-start(bf16[2,48,2304]{2,1,0:T(8,128)(2,1)S(1)} %dynamic-slice_bitcast_fusion.9), channel_id=1, source_target_pairs={{0,2},{1,3},{2,0},{3,1},{4,6},{5,7},{6,4},{7,5},{8,10},{9,11},{10,... | collective-permute-start | bytes 1327112 | tf_op jit(solution)/shard_map/ppermute | solution.py:62
  307.0 12.5 %collective-permute-start.29 = (bf16[2,48,2304]{2,1,0:T(8,128)(2,1)S(1)}, bf16[2,48,2304]{2,1,0:T(8,128)(2,1)S(1)}, u32[]{:S(2)}, u32[]{:S(2)}) collective-permute-start(bf16[2,48,2304]{2,1,0:T(8,128)(2,1)S(1)} %dynamic-slice_bitcast_fusion.8), channel_id=1, source_target_pairs={{0,4},{1,5},{2,6},{3,7},{4,0},{5,1},{6,2},{7,3},{8,12},{9,13},{10,... | collective-permute-start | bytes 1327112 | tf_op jit(solution)/shard_map/ppermute | solution.py:62
  321.6 21.9 %collective-permute-start.57 = (bf16[2,192,768]{2,1,0:T(8,128)(2,1)S(1)}, bf16[2,192,768]{2,1,0:T(8,128)(2,1)S(1)}, u32[]{:S(2)}, u32[]{:S(2)}) collective-permute-start(bf16[2,192,768]{2,1,0:T(8,128)(2,1)S(1)} %dynamic-slice_bitcast_fusion.4), channel_id=1, source_target_pairs={{0,2},{1,3},{2,0},{3,1},{4,6},{5,7},{6,4},{7,5},{8,10},{9,11},{10,... | collective-permute-start | bytes 1769480 | tf_op jit(solution)/shard_map/ppermute | solution.py:62
  322.7 22.3 %collective-permute-start.62 = (bf16[2,192,768]{2,1,0:T(8,128)(2,1)S(1)}, bf16[2,192,768]{2,1,0:T(8,128)(2,1)S(1)}, u32[]{:S(2)}, u32[]{:S(2)}) collective-permute-start(bf16[2,192,768]{2,1,0:T(8,128)(2,1)S(1)} %dynamic-slice_bitcast_fusion.3), channel_id=1, source_target_pairs={{0,4},{1,5},{2,6},{3,7},{4,0},{5,1},{6,2},{7,3},{8,12},{9,13},{10,... | collective-permute-start | bytes 1769480 | tf_op jit(solution)/shard_map/ppermute | solution.py:62
  324.4 21.9 %collective-permute-start.46 = (bf16[2,48,3072]{2,1,0:T(8,128)(2,1)S(1)}, bf16[2,48,3072]{2,1,0:T(8,128)(2,1)S(1)}, u32[]{:S(2)}, u32[]{:S(2)}) collective-permute-start(bf16[2,48,3072]{2,1,0:T(8,128)(2,1)S(1)} %dynamic-slice_bitcast_fusion.6), channel_id=1, source_target_pairs={{0,2},{1,3},{2,0},{3,1},{4,6},{5,7},{6,4},{7,5},{8,10},{9,11},{10,... | collective-permute-start | bytes 1769480 | tf_op jit(solution)/shard_map/ppermute | solution.py:62
  326.1 23.2 %collective-permute-start.51 = (bf16[2,48,3072]{2,1,0:T(8,128)(2,1)S(1)}, bf16[2,48,3072]{2,1,0:T(8,128)(2,1)S(1)}, u32[]{:S(2)}, u32[]{:S(2)}) collective-permute-start(bf16[2,48,3072]{2,1,0:T(8,128)(2,1)S(1)} %dynamic-slice_bitcast_fusion.5), channel_id=1, source_target_pairs={{0,4},{1,5},{2,6},{3,7},{4,0},{5,1},{6,2},{7,3},{8,12},{9,13},{10,... | collective-permute-start | bytes 1769480 | tf_op jit(solution)/shard_map/ppermute | solution.py:62
  342.1 21.8 %collective-permute-start.28 = (bf16[48,2304]{1,0:T(8,128)(2,1)S(1)}, bf16[48,2304]{1,0:T(8,128)(2,1)S(1)}, u32[]{:S(2)}, u32[]{:S(2)}) collective-permute-start(bf16[48,2304]{1,0:T(8,128)(2,1)S(1)} %add_convert_fusion.13), channel_id=1, source_target_pairs={{8,0},{16,24},{9,1},{17,25},{10,2},{18,26},{11,3},{19,27},{12,4},{... | collective-permute-start | bytes 663560 | tf_op jit(solution)/shard_map/ppermute | solution.py:128
  343.5 22.8 %collective-permute-start.33 = (bf16[48,2304]{1,0:T(8,128)(2,1)S(1)}, bf16[48,2304]{1,0:T(8,128)(2,1)S(1)}, u32[]{:S(2)}, u32[]{:S(2)}) collective-permute-start(bf16[48,2304]{1,0:T(8,128)(2,1)S(1)} %add_convert_fusion.11), channel_id=1, source_target_pairs={{8,0},{16,24},{9,1},{17,25},{10,2},{18,26},{11,3},{19,27},{12,4},{... | collective-permute-start | bytes 663560 | tf_op jit(solution)/shard_map/ppermute | solution.py:128
  345.0 23.3 %collective-permute-start.58 = (bf16[192,768]{1,0:T(8,128)(2,1)S(1)}, bf16[192,768]{1,0:T(8,128)(2,1)S(1)}, u32[]{:S(2)}, u32[]{:S(2)}) collective-permute-start(bf16[192,768]{1,0:T(8,128)(2,1)S(1)} %dynamic-slice_bitcast_fusion.11), channel_id=1, source_target_pairs={{0,4},{1,5},{2,6},{3,7},{4,0},{5,1},{6,2},{7,3},{8,12},{9,13},{10,... | collective-permute-start | bytes 884744 | tf_op jit(solution)/shard_map/ppermute | solution.py:62
  346.3 24.3 %collective-permute-start.63 = (bf16[192,768]{1,0:T(8,128)(2,1)S(1)}, bf16[192,768]{1,0:T(8,128)(2,1)S(1)}, u32[]{:S(2)}, u32[]{:S(2)}) collective-permute-start(bf16[192,768]{1,0:T(8,128)(2,1)S(1)} %dynamic-slice_bitcast_fusion.10), channel_id=1, source_target_pairs={{0,2},{1,3},{2,0},{3,1},{4,6},{5,7},{6,4},{7,5},{8,10},{9,11},{10,... | collective-permute-start | bytes 884744 | tf_op jit(solution)/shard_map/ppermute | solution.py:62
  349.3 22.8 %collective-permute-start.47 = (bf16[48,3072]{1,0:T(8,128)(2,1)S(1)}, bf16[48,3072]{1,0:T(8,128)(2,1)S(1)}, u32[]{:S(2)}, u32[]{:S(2)}) collective-permute-start(bf16[48,3072]{1,0:T(8,128)(2,1)S(1)} %dynamic-slice_bitcast_fusion.13), channel_id=1, source_target_pairs={{0,4},{1,5},{2,6},{3,7},{4,0},{5,1},{6,2},{7,3},{8,12},{9,13},{10,... | collective-permute-start | bytes 884744 | tf_op jit(solution)/shard_map/ppermute | solution.py:62
  363.9 9.7 %collective-permute-start.52 = (bf16[48,3072]{1,0:T(8,128)(2,1)S(1)}, bf16[48,3072]{1,0:T(8,128)(2,1)S(1)}, u32[]{:S(2)}, u32[]{:S(2)}) collective-permute-start(bf16[48,3072]{1,0:T(8,128)(2,1)S(1)} %dynamic-slice_bitcast_fusion.12), channel_id=1, source_target_pairs={{0,2},{1,3},{2,0},{3,1},{4,6},{5,7},{6,4},{7,5},{8,10},{9,11},{10,... | collective-permute-start | bytes 884744 | tf_op jit(solution)/shard_map/ppermute | solution.py:62
  372.2 9.0 %collective-permute-start.48 = (bf16[48,3072]{1,0:T(8,128)(2,1)S(1)}, bf16[48,3072]{1,0:T(8,128)(2,1)S(1)}, u32[]{:S(2)}, u32[]{:S(2)}) collective-permute-start(bf16[48,3072]{1,0:T(8,128)(2,1)S(1)} %fusion.29), channel_id=1, source_target_pairs={{0,8},{24,16},{1,9},{25,17},{2,10},{26,18},{3,11},{27,19},{4,12},{... | collective-permute-start | bytes 884744 | tf_op jit(solution)/shard_map/ppermute | solution.py:124
  373.7 10.7 %collective-permute-start.53 = (bf16[48,3072]{1,0:T(8,128)(2,1)S(1)}, bf16[48,3072]{1,0:T(8,128)(2,1)S(1)}, u32[]{:S(2)}, u32[]{:S(2)}) collective-permute-start(bf16[48,3072]{1,0:T(8,128)(2,1)S(1)} %fusion.28), channel_id=1, source_target_pairs={{0,8},{24,16},{1,9},{25,17},{2,10},{26,18},{3,11},{27,19},{4,12},{... | collective-permute-start | bytes 884744 | tf_op jit(solution)/shard_map/ppermute | solution.py:124
  375.1 10.2 %collective-permute-start.60 = (bf16[192,768]{1,0:T(8,128)(2,1)S(1)}, bf16[192,768]{1,0:T(8,128)(2,1)S(1)}, u32[]{:S(2)}, u32[]{:S(2)}) collective-permute-start(bf16[192,768]{1,0:T(8,128)(2,1)S(1)} %add_convert_fusion.6), channel_id=1, source_target_pairs={{8,16},{16,8},{9,17},{17,9},{10,18},{18,10},{11,19},{19,11},{12,20... | collective-permute-start | bytes 884744 | tf_op jit(solution)/shard_map/ppermute | solution.py:125
  378.1 8.7 %collective-permute-start.65 = (bf16[192,768]{1,0:T(8,128)(2,1)S(1)}, bf16[192,768]{1,0:T(8,128)(2,1)S(1)}, u32[]{:S(2)}, u32[]{:S(2)}) collective-permute-start(bf16[192,768]{1,0:T(8,128)(2,1)S(1)} %add_convert_fusion.4), channel_id=1, source_target_pairs={{8,16},{16,8},{9,17},{17,9},{10,18},{18,10},{11,19},{19,11},{12,20... | collective-permute-start | bytes 884744 | tf_op jit(solution)/shard_map/ppermute | solution.py:125
  385.4 11.7 %collective-permute-start.61 = (bf16[192,768]{1,0:T(8,128)(2,1)S(1)}, bf16[192,768]{1,0:T(8,128)(2,1)S(1)}, u32[]{:S(2)}, u32[]{:S(2)}) collective-permute-start(bf16[192,768]{1,0:T(8,128)(2,1)S(1)} %add_convert_fusion.5), channel_id=1, source_target_pairs={{8,0},{16,24},{9,1},{17,25},{10,2},{18,26},{11,3},{19,27},{12,4},{... | collective-permute-start | bytes 884744 | tf_op jit(solution)/shard_map/ppermute | solution.py:128
  386.9 13.4 %collective-permute-start.66 = (bf16[192,768]{1,0:T(8,128)(2,1)S(1)}, bf16[192,768]{1,0:T(8,128)(2,1)S(1)}, u32[]{:S(2)}, u32[]{:S(2)}) collective-permute-start(bf16[192,768]{1,0:T(8,128)(2,1)S(1)} %add_convert_fusion.3), channel_id=1, source_target_pairs={{8,0},{16,24},{9,1},{17,25},{10,2},{18,26},{11,3},{19,27},{12,4},{... | collective-permute-start | bytes 884744 | tf_op jit(solution)/shard_map/ppermute | solution.py:128
  388.3 15.1 %collective-permute-start.50 = (bf16[48,3072]{1,0:T(8,128)(2,1)S(1)}, bf16[48,3072]{1,0:T(8,128)(2,1)S(1)}, u32[]{:S(2)}, u32[]{:S(2)}) collective-permute-start(bf16[48,3072]{1,0:T(8,128)(2,1)S(1)} %add_convert_fusion.9), channel_id=1, source_target_pairs={{8,0},{16,24},{9,1},{17,25},{10,2},{18,26},{11,3},{19,27},{12,4},{... | collective-permute-start | bytes 884744 | tf_op jit(solution)/shard_map/ppermute | solution.py:128
  389.7 16.9 %collective-permute-start.55 = (bf16[48,3072]{1,0:T(8,128)(2,1)S(1)}, bf16[48,3072]{1,0:T(8,128)(2,1)S(1)}, u32[]{:S(2)}, u32[]{:S(2)}) collective-permute-start(bf16[48,3072]{1,0:T(8,128)(2,1)S(1)} %add_convert_fusion.7), channel_id=1, source_target_pairs={{8,0},{16,24},{9,1},{17,25},{10,2},{18,26},{11,3},{19,27},{12,4},{... | collective-permute-start | bytes 884744 | tf_op jit(solution)/shard_map/ppermute | solution.py:128
  (98 other events, 903.6 us)

commit v2 on v1

--- a/solution.py
+++ b/solution.py
@@ -82,15 +82,48 @@
     return value, held_bits
 
 
+class Pipe:
+    def __init__(self, stages):
+        self.stages = stages
+        self.state = next(stages)
+        self.done = False
+
+    def advance(self):
+        try:
+            self.state = self.stages.send(self.state)
+        except StopIteration as end:
+            self.state, self.done = end.value, True
+
+
+def tick(pipes, values):
+    active = [pipe for pipe in pipes if not pipe.done]
+    for pipe in active:
+        pipe.advance()
+    values, states = lax.optimization_barrier((values, [pipe.state for pipe in active]))
+    for pipe, state in zip(active, states):
+        pipe.state = state
+    return values
+
+
+def drain(pipes, values):
+    while not all(pipe.done for pipe in pipes):
+        values = tick(pipes, values)
+    return values
+
+
 def gather_rows(block):
     size = lax.axis_size("zero")
     rows, columns = block.shape
     low = block.astype(jnp.bfloat16)
     order_one, order_two = bit_orders(size)
-    part_one, held = gather_bits(low[: rows // 2], [], order_one[::-1], size)
-    part_two, _ = gather_bits(low[rows // 2 :], [], order_two[::-1], size)
-    whole = jnp.concatenate([part_one, part_two], axis=-2)
-    whole, _ = gather_bits(whole, held, [0], size)
+    parts = yield (low[: rows // 2], low[rows // 2 :])
+    held_one, held_two = [], []
+    for bit_one, bit_two in zip(order_one[::-1], order_two[::-1]):
+        part_one, held_one = gather_bits(parts[0], held_one, [bit_one], size)
+        part_two, held_two = gather_bits(parts[1], held_two, [bit_two], size)
+        parts = yield (part_one, part_two)
+    whole = jnp.concatenate(parts, axis=-2)
+    whole, _ = gather_bits(whole, held_one, [0], size)
     return whole.reshape(size * rows, columns)
 
 
@@ -108,26 +141,28 @@
     return value, held_bits
 
 
-def sum_line(value):
+def sum_line(values):
     count = lax.axis_size("dp")
     if count % 2 == 1:
-        return lax.psum(value.astype(jnp.float32), "dp")
+        return [lax.psum(value.astype(jnp.float32), "dp") for value in values]
     index = lax.axis_index("dp")
     half = count // 2
 
     def add(left, right):
-        return (left.astype(jnp.float32) + right.astype(jnp.float32)).astype(value.dtype)
-
-    total = value
+        return (left.astype(jnp.float32) + right.astype(jnp.float32)).astype(left.dtype)
+
     for step in range(half - 1):
         pairs = [(step, step + 1), (count - 1 - step, count - 2 - step)]
-        total = add(total, lax.ppermute(total, "dp", pairs))
-    total = add(total, lax.ppermute(total, "dp", [(half - 1, half), (half, half - 1)]))
+        values = yield [add(value, lax.ppermute(value, "dp", pairs)) for value in values]
+    pairs = [(half - 1, half), (half, half - 1)]
+    values = yield [add(value, lax.ppermute(value, "dp", pairs)) for value in values]
     for step in range(half - 2, -1, -1):
         pairs = [(step + 1, step), (count - 2 - step, count - 1 - step)]
-        came = lax.ppermute(total, "dp", pairs)
-        total = jnp.where((index == step) | (index == count - 1 - step), came, total)
-    return total.astype(jnp.float32)
+        outer = (index == step) | (index == count - 1 - step)
+        values = yield [
+            jnp.where(outer, lax.ppermute(value, "dp", pairs), value) for value in values
+        ]
+    return [value.astype(jnp.float32) for value in values]
 
 
 def reduce_rows(partial_sum):
@@ -137,17 +172,28 @@
     bits = size.bit_length() - 1
     held = list(range(bits - 1, -1, -1))
     order_one, order_two = bit_orders(size)
-    value = partial_sum.reshape((2,) * bits + (rows, columns))
+    value = yield partial_sum.reshape((2,) * bits + (rows, columns))
     value, held = halve_bits(value, held, [0], size)
-    part_one, _ = halve_bits(value[..., : rows // 2, :], held, order_one, size)
-    part_two, _ = halve_bits(value[..., rows // 2 :, :], held, order_two, size)
-    return jnp.concatenate([sum_line(part_one), sum_line(part_two)], axis=0)
+    value = yield value
+    parts = (value[..., : rows // 2, :], value[..., rows // 2 :, :])
+    held_one, held_two = held, held
+    for bit_one, bit_two in zip(order_one, order_two):
+        part_one, held_one = halve_bits(parts[0], held_one, [bit_one], size)
+        part_two, held_two = halve_bits(parts[1], held_two, [bit_two], size)
+        parts = yield (part_one, part_two)
+    parts = yield from sum_line(list(parts))
+    return jnp.concatenate(parts, axis=0)
 
 
 def gather_vectors(block):
     size = lax.axis_size("zero")
     order_one, _ = bit_orders(size)
-    whole, _ = gather_bits(block.astype(jnp.bfloat16), [], order_one[::-1] + [0], size)
+    whole = yield block.astype(jnp.bfloat16)
+    held = []
+    for bit in order_one[::-1]:
+        whole, held = gather_bits(whole, held, [bit], size)
+        whole = yield whole
+    whole, held = gather_bits(whole, held, [0], size)
     rows, columns = block.shape
     return whole.reshape(size, rows, columns).transpose(1, 0, 2).reshape(rows, size * columns)
 
@@ -158,9 +204,13 @@
     bits = size.bit_length() - 1
     order_one, _ = bit_orders(size)
     value = partial_sum.reshape(rows, size, columns // size).transpose(1, 0, 2)
-    value = value.reshape((2,) * bits + (rows, columns // size))
-    value, _ = halve_bits(value, list(range(bits - 1, -1, -1)), [0] + order_one, size)
-    return sum_line(value)
+    value = yield value.reshape((2,) * bits + (rows, columns // size))
+    held = list(range(bits - 1, -1, -1))
+    for bit in [0] + order_one:
+        value, held = halve_bits(value, held, [bit], size)
+        value = yield value
+    (value,) = yield from sum_line([value])
+    return value
 
 
 def contract(left_side, right_side, left_dim, right_dim):
@@ -304,11 +354,11 @@
     second_fc2,
     second_vectors,
 ):
-    vectors = gather_vectors(master_vectors).astype(jnp.float32)
-    w_qkv = gather_rows(master_qkv)
-    w_proj = gather_rows(master_proj)
-    w_fc1 = gather_rows(master_fc1)
-    w_fc2 = gather_rows(master_fc2)
+    get_vectors = Pipe(gather_vectors(master_vectors))
+    get_qkv = Pipe(gather_rows(master_qkv))
+    get_proj = Pipe(gather_rows(master_proj))
+    get_fc1 = Pipe(gather_rows(master_fc1))
+    get_fc2 = Pipe(gather_rows(master_fc2))
     slot_count, length, feature_width = images.shape
     padded = -(-length // 16) * 16
     row_count = slot_count * padded
@@ -322,6 +372,14 @@
         jnp.pad(images, more_rows).astype(jnp.float32).reshape(row_count, feature_width)
     )
     normed_one, inverse_one = layer_stats(inputs)
+    tick([get_qkv, get_vectors], ())
+    normed_one, inverse_one = tick(
+        [get_qkv, get_vectors, get_proj], (normed_one, inverse_one)
+    )
+    while not get_qkv.done:
+        tick([get_qkv, get_vectors, get_proj, get_fc1], ())
+    w_qkv = get_qkv.state
+    vectors = get_vectors.state.astype(jnp.float32)
     hidden_one = (normed_one * vectors[0] + vectors[1]).astype(jnp.bfloat16)
     joined_bias = jnp.concatenate([vectors[2], jnp.zeros_like(vectors[2]), vectors[3]])
     joined = (
@@ -330,41 +388,54 @@
         .reshape(slot_count, padded, 3 * feature_width)
     )
     attn_slots, log_total = attend(joined, length, score_scale, 16)
+    attn_slots, log_total = tick([get_proj, get_fc1, get_fc2], (attn_slots, log_total))
+    drain([get_proj], ())
+    w_proj = get_proj.state
     attn_low = attn_slots.reshape(row_count, feature_width)
     mixed_rows = inputs + jnp.dot(attn_low, w_proj, preferred_element_type=jnp.float32) + vectors[4]
     normed_two, inverse_two = layer_stats(mixed_rows)
     hidden_two = (normed_two * vectors[5] + vectors[6]).astype(jnp.bfloat16)
+    hidden_two = drain([get_fc1], hidden_two)
+    w_fc1 = get_fc1.state
     fc1_bias = vectors[8:].reshape(-1)
     pre_act = jnp.dot(hidden_two, w_fc1, preferred_element_type=jnp.float32) + fc1_bias
     act_value, gelu_back = jax.vjp(partial(jax.nn.gelu, approximate=False), pre_act)
     act_low = act_value.astype(jnp.bfloat16)
-    block_rows = (
-        mixed_rows + jnp.dot(act_low, w_fc2, preferred_element_type=jnp.float32) + vectors[7]
-    )
-    block_out = (block_rows * row_live).astype(jnp.bfloat16).reshape(slot_shape)[:, :length]
+    while not get_fc2.done:
+        get_fc2.advance()
+    act_low, w_fc2 = lax.optimization_barrier((act_low, get_fc2.state))
     grad_rows = (
         jnp.pad(cotangent, more_rows).astype(jnp.float32).reshape(row_count, feature_width)
         * row_live
     )
     grad_low = grad_rows.astype(jnp.bfloat16)
-    sum_fc2 = reduce_rows(left_product(act_low, grad_low).astype(jnp.bfloat16))
+    partial_fc2 = left_product(act_low, grad_low).astype(jnp.bfloat16)
+    partial_fc2, grad_low = lax.optimization_barrier((partial_fc2, grad_low))
+    put_fc2 = Pipe(reduce_rows(partial_fc2))
     bias_fc2 = jnp.sum(grad_low.astype(jnp.float32), 0)
     grad_pre = gelu_back(right_product(grad_low, w_fc2))[0]
-    pre_low = grad_pre.astype(jnp.bfloat16)
-    sum_fc1 = reduce_rows(left_product(hidden_two, pre_low).astype(jnp.bfloat16))
+    pre_low = tick([put_fc2], grad_pre.astype(jnp.bfloat16))
+    partial_fc1 = left_product(hidden_two, pre_low).astype(jnp.bfloat16)
+    partial_fc1, pre_low = tick([put_fc2], (partial_fc1, pre_low))
+    put_fc1 = Pipe(reduce_rows(partial_fc1))
     bias_fc1 = jnp.sum(pre_low.astype(jnp.float32), 0)
     back_two = right_product(pre_low, w_fc1)
     gain_two = jnp.sum(back_two * normed_two, 0)
     shift_two = jnp.sum(back_two, 0)
     grad_mixed = grad_rows + norm_back(back_two, normed_two, inverse_two, vectors[5])
     mixed_low = grad_mixed.astype(jnp.bfloat16)
-    sum_proj = reduce_rows(left_product(attn_low, mixed_low).astype(jnp.bfloat16))
+    mixed_low = tick([put_fc2, put_fc1], mixed_low)
+    partial_proj = left_product(attn_low, mixed_low).astype(jnp.bfloat16)
     bias_proj = jnp.sum(mixed_low.astype(jnp.float32), 0)
     back_attn = right_product(mixed_low, w_proj).astype(jnp.bfloat16).reshape(slot_shape)
     grad_joined = attend_back(joined, log_total, back_attn, length, score_scale).reshape(
         row_count, 3 * feature_width
     )
-    sum_qkv = reduce_rows(left_product(hidden_one, grad_joined).astype(jnp.bfloat16))
+    partial_proj, grad_joined = tick([put_fc2, put_fc1], (partial_proj, grad_joined))
+    put_proj = Pipe(reduce_rows(partial_proj))
+    partial_qkv = left_product(hidden_one, grad_joined).astype(jnp.bfloat16)
+    partial_qkv, grad_joined = tick([put_fc2, put_fc1, put_proj], (partial_qkv, grad_joined))
+    put_qkv = Pipe(reduce_rows(partial_qkv))
     bias_query = jnp.sum(grad_joined[:, :feature_width].astype(jnp.float32), 0)
     bias_value = jnp.sum(grad_joined[:, 2 * feature_width :].astype(jnp.float32), 0)
     back_one = right_product(grad_joined, w_qkv)
@@ -391,7 +462,18 @@
         ],
         0,
     )
-    sum_vectors = reduce_vectors(grad_vectors)
+    act_low, grad_vectors = tick(
+        [put_fc2, put_fc1, put_proj, put_qkv], (act_low, grad_vectors)
+    )
+    put_vectors = Pipe(reduce_vectors(grad_vectors))
+    block_rows = (
+        mixed_rows + jnp.dot(act_low, w_fc2, preferred_element_type=jnp.float32) + vectors[7]
+    )
+    block_out = (block_rows * row_live).astype(jnp.bfloat16).reshape(slot_shape)[:, :length]
+    drain([put_fc2, put_fc1, put_proj, put_qkv, put_vectors], ())
+    sum_fc2, sum_fc1, sum_proj, sum_qkv, sum_vectors = (
+        pipe.state for pipe in (put_fc2, put_fc1, put_proj, put_qkv, put_vectors)
+    )
     new_qkv = adamw(sum_qkv, first_qkv, second_qkv, master_qkv, RATE_MATRIX, DECAY_MATRIX)
     new_proj = adamw(sum_proj, first_proj, second_proj, master_proj, RATE_MATRIX, DECAY_MATRIX)
     new_fc1 = adamw(sum_fc1, first_fc1, second_fc1, master_fc1, RATE_MATRIX, DECAY_MATRIX)

time: 418 us -> 426 us (1.019)
  waiting for transfers between devices: 117 us -> 78.6 us
  starting transfers between devices: 77.5 us -> 108 us
  other arithmetic: 51.2 us -> 74.5 us
  matrix products: 115 us -> 101 us
  local copies, waits for them, and re-layouts: 22.1 us -> 28.9 us
    ppermute x27, starting transfers between devices: 39.6 us -> 64.1 us  [sum_line(): lax.ppermute(value, 'dp', pairs)]
    ppermute x46, waiting for transfers between devices: 58.8 us -> 34.4 us  [swap(): return lax.ppermute(value, axis, [(i, i ^ 1 << bit) for i in range(size)])]
    ppermute x27, waiting for transfers between devices: 58.3 us -> 44.2 us  [sum_line(): lax.ppermute(value, 'dp', pairs)]
    convert_element_type x20, other arithmetic: 4.64 us -> 16.5 us  [halve_bits(): (kept.astype(jnp.float32) + came.astype(jnp.float32)).astype(value.dtype)]
    convert_element_type x19 -> x21, other arithmetic: 3.28 us -> 10.8 us  [the longest x16 5.12 us: add(): (left.astype(jnp.float32) + right.astype(jnp.float32)).astype(left.dtype)]
    dot_general x4, matrix products: 34.7 us -> 27.6 us  [right_product(): lax.dot_general(left_side, right_side, (((1,), (1,)), ((), ())), preferre...]
    dot_general x4, matrix products: 27 us -> 21 us  [left_product(): lax.dot_general(left_side, right_side, (((0,), (0,)), ((), ())), preferre...]
    ppermute x46, starting transfers between devices: 37.9 us -> 43.5 us  [swap(): return lax.ppermute(value, axis, [(i, i ^ 1 << bit) for i in range(size)])]
  transfers between devices with their start and end apart: 73 -> 73, of which waited for: 33 -> 19; matrix products, arithmetic and copies ran while one was open for 20% -> 39% of each run, Pallas kernels for 2% -> 6%
where the time goes in v2:
time: 426 us; the launch traced here: 419 us
  starting transfers between devices  108 us (25%)
  matrix products  101 us (24%)
  waiting for transfers between devices  78.6 us (18%)
  other arithmetic  74.5 us (17%)
  local copies, waits for them, and re-layouts  28.9 us (7%)
  Pallas kernels  24.2 us (6%)
    ppermute x27, starting transfers between devices, sum_line(): lax.ppermute(value, 'dp', pairs)  64.1 us
    ppermute x27, waiting for transfers between devices, sum_line(): lax.ppermute(value, 'dp', pairs)  44.2 us
    ppermute x46, starting transfers between devices, swap(): return lax.ppermute(value, axis, [(i, i ^ 1 << bit) for i in range(size)])  43.5 us
    dot_general x1, matrix products, per_device(): jnp.dot(hidden_two, w_fc1, preferred_element_type=jnp.float32) + fc1_bias  36.7 us
    ppermute x46, waiting for transfers between devices, swap(): return lax.ppermute(value, axis, [(i, i ^ 1 << bit) for i in range(size)])  34.4 us
    dot_general x4, matrix products, right_product(): lax.dot_general(left_side, right_side, (((1,), (1,)), ((), ())), preferre...  27.6 us
    dot_general x4, matrix products, left_product(): lax.dot_general(left_side, right_side, (((0,), (0,)), ((), ())), preferre...  21 us
    another operation x36, other arithmetic, gather_bits(): jnp.stack([jnp.where(first, value, other), jnp.where(first, other, value)...  19.5 us
  transfers between devices with their start and end apart: 73, of which 19 were waited for; matrix products, arithmetic and copies ran while one was open for 39% of the time, Pallas kernels for 6%

profile of v2, /device:TPU:0, one launch (start us, length us, event | category | flops | bytes accessed | tf_op | source)
XLA Modules:
  0.0 419.4 jit_solution(11236777128445840211)
XLA Ops:
  2.7 3.0 collective-permute-start
  13.1 2.0 pad_convert_fusion
  22.3 3.0 fusion.16
  29.0 2.0 collective-permute-start.13
  36.9 6.0 %collective-permute-done.5 = bf16[2,12,96]{2,1,0:T(8,128)(2,1)S(1)} collective-permute-done((bf16[2,12,96]{2,1,0:T(8,128)(2,1)S(1)}, bf16[2,12,96]{2,1,0:T(8,128)(2,1)S(1)}, u32[]{:S(2)}, u32[]{:S(2)}) %collective-permute-start.5) | collective-permute-done | bytes 4640 | tf_op jit(solution)/shard_map/ppermute | solution.py:62
  46.3 6.2 %collective-permute-done.4 = bf16[2,48,2304]{2,1,0:T(8,128)(2,1)S(1)} collective-permute-done((bf16[2,48,2304]{2,1,0:T(8,128)(2,1)S(1)}, bf16[2,48,2304]{2,1,0:T(8,128)(2,1)S(1)}, u32[]{:S(2)}, u32[]{:S(2)}) %collective-permute-start.4) | collective-permute-done | bytes 442400 | tf_op jit(solution)/shard_map/ppermute | solution.py:62
  58.8 3.1 collective-permute-done.11
  69.4 5.9 %fusion.6 = bf16[1040,2304]{1,0:T(8,128)(2,1)} fusion(bf16[768,2304]{1,0:T(8,128)(2,1)S(1)} %bitcast.297, f32[2304]{0:T(1024)S(1)} %pad_maximum_fusion.21, f32[1040,768]{1,0:T(8,128)S(1)} %copy-done.8, f32[768]{0:T(1024)S(1)} %get-tuple-element.228, f32[768]{0:T(1024)S(1)} %get-tuple-element.229), kind=kOutput, calls=%fused_computation.20 | convolution fusion | flops 3687690240 | bytes 11541504 | tf_op jit(solution)/shard_map/dot_general | solution.py:386
  75.3 2.3 copy-done
  77.7 8.1 %attend.1 = (bf16[5,208,768]{2,1,0:T(8,128)(2,1)S(1)}, f32[5,16,208]{2,1,0:T(8,128)S(1)}) custom-call(bf16[5,208,2304]{2,1,0:T(8,128)(2,1)S(1)} %bitcast.279), custom_call_target="tpu_custom_call" | custom-call | flops 2658140160 | bytes 6389760 | tf_op jit(solution)/shard_map/attend/pallas_call | solution.py:295
  96.1 10.2 %collective-permute-done.20 = bf16[2,192,768]{2,1,0:T(8,128)(2,1)S(1)} collective-permute-done((bf16[2,192,768]{2,1,0:T(8,128)(2,1)S(1)}, bf16[2,192,768]{2,1,0:T(8,128)(2,1)S(1)}, u32[]{:S(2)}, u32[]{:S(2)}) %collective-permute-start.20) | collective-permute-done | bytes 589856 | tf_op jit(solution)/shard_map/ppermute | solution.py:62
  106.6 1.8 maximum_maximum_fusion
  109.3 36.7 %multiply_convert_fusion = (bf16[1040,3072]{1,0:T(8,128)(2,1)S(1)}, f32[1040,3072]{1,0:T(8,128)}, f32[1040,3072]{1,0:T(8,128)}) fusion(f32[3072]{0:T(1024)S(1)} %add.388, bf16[1040,768]{1,0:T(8,128)(2,1)S(1)} %add_convert_fusion.1, bf16[768,3072]{1,0:T(8,128)(2,1)S(1)} %bitcast.293), kind=kOutput, calls=%fused_computation.6 | convolution fusion | flops 5118197760 | bytes 38277120 | tf_op jit(solution)/shard_map/dot_general | solution.py:401
  146.1 3.9 select_bitcast_fusion.1
  150.0 2.5 pad_maximum_fusion.1
  152.5 7.3 %convolution_convert_fusion.2 = bf16[3072,768]{1,0:T(8,128)(2,1)S(1)} fusion(bf16[1040,3072]{1,0:T(8,128)(2,1)S(1)} %get-tuple-element.170, bf16[1040,768]{1,0:T(8,128)(2,1)S(1)} %copy-done.13), kind=kOutput, calls=%fused_computation.23 | convolution fusion | flops 4909694976 | bytes 12705792 | tf_op jit(solution)/shard_map/dot_general | solution.py:39
  162.1 15.7 %add_convert_fusion = bf16[1040,3072]{1,0:T(8,128)(2,1)} fusion(f32[1040,3072]{1,0:T(8,128)} %get-tuple-element.248, bf16[1040,768]{1,0:T(8,128)(2,1)S(1)} %copy-done.13, bf16[3072,768]{1,0:T(8,128)(2,1)} %bitcast.291, f32[1040,3072]{1,0:T(8,128)} %get-tuple-element.327), kind=kOutput, calls=%fused_computation.5 | convolution fusion | flops 4952064000 | bytes 38264832 | tf_op jit(solution)/shard_map/dot_general | solution.py:45
  177.9 2.3 fusion.8
  183.4 6.8 %convolution_convert_fusion.1 = bf16[768,3072]{1,0:T(8,128)(2,1)S(1)} fusion(bf16[1040,768]{1,0:T(8,128)(2,1)S(1)} %copy-done.38, bf16[1040,3072]{1,0:T(8,128)(2,1)S(1)} %copy-done.12), kind=kOutput, calls=%fused_computation.22 | convolution fusion | flops 4909694976 | bytes 12705792 | tf_op jit(solution)/shard_map/dot_general | solution.py:39
  190.2 5.7 %collective-permute-done.25 = bf16[2,192,768]{2,1,0:T(8,128)(2,1)S(1)} collective-permute-done((bf16[2,192,768]{2,1,0:T(8,128)(2,1)S(1)}, bf16[2,192,768]{2,1,0:T(8,128)(2,1)S(1)}, u32[]{:S(2)}, u32[]{:S(2)}) %collective-permute-start.25) | collective-permute-done | bytes 589856 | tf_op jit(solution)/shard_map/ppermute | solution.py:62
  202.4 5.9 %multiply_reduce_fusion.1 = (f32[768]{0:T(1024)S(1)}, f32[1040]{0:T(1024)S(1)}, f32[1040]{0:T(1024)S(1)}, f32[768]{0:T(1024)S(1)}, f32[1040,768]{1,0:T(8,128)S(1)}) fusion(f32[1040,768]{1,0:T(8,128)S(1)} %copy-done.4, f32[1040]{0:T(1024)S(1)} %copy-done.66, f32[1040]{0:T(1024)S(1)} %copy-done.62, f32[768]{0:T(1024)S(1)} %copy-done.70, ...), kind=kOutput, calls=%fused_computation.48 | convolution fusion | flops 4914520064 | bytes 17523968 | tf_op jit(solution)/shard_map/dot_general | solution.py:45
  208.4 2.9 fusion.44
  214.5 3.3 fusion.7
  220.3 3.6 collective-permute-start.30
  226.8 16.1 %attend_back.1 = bf16[5,208,2304]{2,1,0:T(8,128)(2,1)S(1)} custom-call(bf16[5,208,2304]{2,1,0:T(8,128)(2,1)S(1)} %bitcast.282, f32[5,16,208]{2,1,0:T(8,128)S(1)} %get-tuple-element.153.lse_ref, bf16[5,208,768]{2,1,0:T(8,128)(2,1)S(1)} %bitcast.285), custom_call_target="tpu_custom_call" | custom-call | flops 6645350400 | bytes 11182080 | tf_op jit(solution)/shard_map/attend_back/pallas_call | solution.py:317
  242.9 1.8 convolution_convert_fusion.4
  249.1 5.1 %convolution_convert_fusion = bf16[768,2304]{1,0:T(8,128)(2,1)S(1)} fusion(bf16[1040,2304]{1,0:T(8,128)(2,1)S(1)} %bitcast.276, f32[1040,768]{1,0:T(8,128)S(1)} %copy-done.9, f32[768]{0:T(1024)S(1)} %copy-done.81, f32[768]{0:T(1024)S(1)} %copy-done.74), kind=kOutput, calls=%fused_computation.21 | convolution fusion | flops 3684667392 | bytes 11532288 | tf_op jit(solution)/shard_map/dot_general | solution.py:39
  262.9 10.8 %collective-permute-start.41 = (bf16[48,3072]{1,0:T(8,128)(2,1)S(1)}, bf16[48,3072]{1,0:T(8,128)(2,1)}, u32[]{:S(2)}, u32[]{:S(2)}) collective-permute-start(bf16[48,3072]{1,0:T(8,128)(2,1)S(1)} %fusion.27), channel_id=1, source_target_pairs={{0,8},{24,16},{1,9},{25,17},{2,10},{26,18},{3,11},{27,19},{4,12},{... | collective-permute-start | bytes 884744 | tf_op jit(solution)/shard_map/ppermute | solution.py:156
  273.6 2.0 collective-permute-start.40
  275.6 4.5 %multiply_reduce_fusion = (f32[1040]{0:T(1024)S(1)}, f32[768]{0:T(1024)S(1)}, f32[1040]{0:T(1024)S(1)}, f32[768]{0:T(1024)S(1)}, f32[1040,768]{1,0:T(8,128)S(1)}) fusion(f32[1040,768]{1,0:T(8,128)S(1)} %copy-done.9, f32[768]{0:T(1024)S(1)} %copy-done.74, bf16[1040,2304]{1,0:T(8,128)(2,1)S(1)} %bitcast.277, bf16[768,2304]{1,0:T(8,128)(2,1)S(1)} %bitcast.298), kind=kOutput, calls=%fused_computation.46 | convolution fusion | flops 3686089216 | bytes 14738560 | tf_op jit(solution)/shard_map/dot_general | solution.py:45
  283.2 1.9 slice.136
  292.6 1.7 add_convert_fusion.5
  294.4 4.3 %collective-permute-done.39 = bf16[192,768]{1,0:T(8,128)(2,1)S(1)} collective-permute-done((bf16[192,768]{1,0:T(8,128)(2,1)}, bf16[192,768]{1,0:T(8,128)(2,1)S(1)}, u32[]{:S(2)}, u32[]{:S(2)}) %collective-permute-start.39) | collective-permute-done | bytes 294944 | tf_op jit(solution)/shard_map/ppermute | solution.py:163
  299.4 4.3 %collective-permute-done.38 = bf16[192,768]{1,0:T(8,128)(2,1)S(1)} collective-permute-done((bf16[192,768]{1,0:T(8,128)(2,1)}, bf16[192,768]{1,0:T(8,128)(2,1)S(1)}, u32[]{:S(2)}, u32[]{:S(2)}) %collective-permute-start.38) | collective-permute-done | bytes 294944 | tf_op jit(solution)/shard_map/ppermute | solution.py:163
  305.6 3.2 fusion.12
  315.9 8.7 %fusion.13 = bf16[1040,768]{1,0:T(8,128)(2,1)S(1)} fusion(f32[1040,768]{1,0:T(8,128)S(1)} %copy-done.4, bf16[1040,3072]{1,0:T(8,128)(2,1)} %copy-done.82, bf16[3072,768]{1,0:T(8,128)(2,1)} %bitcast.292, f32[768]{0:T(1024)S(1)} %copy-done.79, f32[1040]{0:T(1024)S(1)} %copy-done.64), kind=kOutput, calls=%fused_computation.38 | convolution fusion | flops 4910530560 | bytes 15907904 | tf_op jit(solution)/shard_map/dot_general | solution.py:470
  331.1 17.3 %collective-permute-start.55 = (bf16[48,768]{1,0:T(8,128)(2,1)S(1)}, bf16[48,768]{1,0:T(8,128)(2,1)S(1)}, u32[]{:S(2)}, u32[]{:S(2)}) collective-permute-start(bf16[48,768]{1,0:T(8,128)(2,1)S(1)} %fusion.36), channel_id=1, source_target_pairs={{0,8},{24,16},{1,9},{25,17},{2,10},{26,18},{3,11},{27,19},{4,12},{... | collective-permute-start | bytes 221192 | tf_op jit(solution)/shard_map/ppermute | solution.py:156
  352.5 8.4 %collective-permute-done.53 = bf16[48,3072]{1,0:T(8,128)(2,1)S(1)} collective-permute-done((bf16[48,3072]{1,0:T(8,128)(2,1)S(1)}, bf16[48,3072]{1,0:T(8,128)(2,1)S(1)}, u32[]{:S(2)}, u32[]{:S(2)}) %collective-permute-start.53) | collective-permute-done | bytes 294944 | tf_op jit(solution)/shard_map/ppermute | solution.py:163
  360.9 3.1 collective-permute-done.52
  370.5 2.3 collective-permute-done.61
  372.9 6.9 %collective-permute-start.68 = (f32[12,96]{1,0:T(8,128)S(1)}, f32[12,96]{1,0:T(8,128)S(1)}, u32[]{:S(2)}, u32[]{:S(2)}) collective-permute-start(f32[12,96]{1,0:T(8,128)S(1)} %bitcast_add_fusion.2), channel_id=1, source_target_pairs={{0,8},{24,16},{1,9},{25,17},{2,10},{26,18},{3,11},{27,19},{4,12},{... | collective-permute-start | bytes 13832 | tf_op jit(solution)/shard_map/ppermute | solution.py:156
  381.2 2.3 multiply_subtract_fusion
  386.2 10.2 %collective-permute-done.64 = bf16[48,768]{1,0:T(8,128)(2,1)S(1)} collective-permute-done((bf16[48,768]{1,0:T(8,128)(2,1)S(1)}, bf16[48,768]{1,0:T(8,128)(2,1)S(1)}, u32[]{:S(2)}, u32[]{:S(2)}) %collective-permute-start.64) | collective-permute-done | bytes 73760 | tf_op jit(solution)/shard_map/ppermute | solution.py:163
  397.9 2.4 multiply_subtract_fusion.1
  402.6 1.8 collective-permute-done.70
  404.4 6.4 %collective-permute-done.69 = bf16[48,2304]{1,0:T(8,128)(2,1)S(1)} collective-permute-done((bf16[48,2304]{1,0:T(8,128)(2,1)S(1)}, bf16[48,2304]{1,0:T(8,128)(2,1)S(1)}, u32[]{:S(2)}, u32[]{:S(2)}) %collective-permute-start.69) | collective-permute-done | bytes 221216 | tf_op jit(solution)/shard_map/ppermute | solution.py:163
  413.4 2.9 collective-permute-done.72
  416.4 1.9 multiply_subtract_fusion.2
  (479 shorter events, 134.9 us)
Async XLA Ops:
  2.7 30.8 %collective-permute-start = (bf16[48,2304]{1,0:T(8,128)(2,1)}, bf16[48,2304]{1,0:T(8,128)(2,1)}, u32[]{:S(2)}, u32[]{:S(2)}) collective-permute-start(bf16[48,2304]{1,0:T(8,128)(2,1)} %get-tuple-element.300), channel_id=1, source_target_pairs={{0,4},{1,5},{2,6},{3,7},{4,0},{5,1},{6,2},{7,3},{8,12},{9,13},{10,... | collective-permute-start | bytes 663560 | tf_op jit(solution)/shard_map/ppermute | solution.py:62
  5.7 28.5 %collective-permute-start.1 = (bf16[48,2304]{1,0:T(8,128)(2,1)S(1)}, bf16[48,2304]{1,0:T(8,128)(2,1)}, u32[]{:S(2)}, u32[]{:S(2)}) collective-permute-start(bf16[48,2304]{1,0:T(8,128)(2,1)S(1)} %get-tuple-element.299), channel_id=1, source_target_pairs={{0,2},{1,3},{2,0},{3,1},{4,6},{5,7},{6,4},{7,5},{8,10},{9,11},{10,... | collective-permute-start | bytes 663560 | tf_op jit(solution)/shard_map/ppermute | solution.py:62
  7.9 20.3 %collective-permute-start.2 = (bf16[12,96]{1,0:T(8,128)(2,1)S(1)}, bf16[12,96]{1,0:T(8,128)(2,1)}, u32[]{:S(2)}, u32[]{:S(2)}) collective-permute-start(bf16[12,96]{1,0:T(8,128)(2,1)S(1)} %convert_element_type.476), channel_id=1, source_target_pairs={{0,4},{1,5},{2,6},{3,7},{4,0},{5,1},{6,2},{7,3},{8,12},{9,13},{10,... | collective-permute-start | bytes 6920 | tf_op jit(solution)/shard_map/ppermute | solution.py:62
  10.0 19.0 %collective-permute-start.6 = (bf16[48,768]{1,0:T(8,128)(2,1)}, bf16[48,768]{1,0:T(8,128)(2,1)}, u32[]{:S(2)}, u32[]{:S(2)}) collective-permute-start(bf16[48,768]{1,0:T(8,128)(2,1)} %get-tuple-element.312), channel_id=1, source_target_pairs={{0,4},{1,5},{2,6},{3,7},{4,0},{5,1},{6,2},{7,3},{8,12},{9,13},{10,... | collective-permute-start | bytes 221192 | tf_op jit(solution)/shard_map/ppermute | solution.py:62
  11.6 19.5 %collective-permute-start.7 = (bf16[48,768]{1,0:T(8,128)(2,1)}, bf16[48,768]{1,0:T(8,128)(2,1)}, u32[]{:S(2)}, u32[]{:S(2)}) collective-permute-start(bf16[48,768]{1,0:T(8,128)(2,1)} %get-tuple-element.311), channel_id=1, source_target_pairs={{0,2},{1,3},{2,0},{3,1},{4,6},{5,7},{6,4},{7,5},{8,10},{9,11},{10,... | collective-permute-start | bytes 221192 | tf_op jit(solution)/shard_map/ppermute | solution.py:62
  28.2 16.5 %collective-permute-start.12 = (bf16[48,3072]{1,0:T(8,128)(2,1)}, bf16[48,3072]{1,0:T(8,128)(2,1)S(1)}, u32[]{:S(2)}, u32[]{:S(2)}) collective-permute-start(bf16[48,3072]{1,0:T(8,128)(2,1)} %get-tuple-element.296), channel_id=1, source_target_pairs={{0,4},{1,5},{2,6},{3,7},{4,0},{5,1},{6,2},{7,3},{8,12},{9,13},{10,... | collective-permute-start | bytes 884744 | tf_op jit(solution)/shard_map/ppermute | solution.py:62
  29.0 17.2 %collective-permute-start.13 = (bf16[48,3072]{1,0:T(8,128)(2,1)S(1)}, bf16[48,3072]{1,0:T(8,128)(2,1)S(1)}, u32[]{:S(2)}, u32[]{:S(2)}) collective-permute-start(bf16[48,3072]{1,0:T(8,128)(2,1)S(1)} %copy-done.60), channel_id=1, source_target_pairs={{0,2},{1,3},{2,0},{3,1},{4,6},{5,7},{6,4},{7,5},{8,10},{9,11},{10,... | collective-permute-start | bytes 884744 | tf_op jit(solution)/shard_map/ppermute | solution.py:62
  31.1 23.1 %collective-permute-start.17 = (bf16[192,768]{1,0:T(8,128)(2,1)}, bf16[192,768]{1,0:T(8,128)(2,1)S(1)}, u32[]{:S(2)}, u32[]{:S(2)}) collective-permute-start(bf16[192,768]{1,0:T(8,128)(2,1)} %get-tuple-element.292), channel_id=1, source_target_pairs={{0,4},{1,5},{2,6},{3,7},{4,0},{5,1},{6,2},{7,3},{8,12},{9,13},{10,... | collective-permute-start | bytes 884744 | tf_op jit(solution)/shard_map/ppermute | solution.py:62
  33.6 20.6 %collective-permute-start.18 = (bf16[192,768]{1,0:T(8,128)(2,1)S(1)}, bf16[192,768]{1,0:T(8,128)(2,1)S(1)}, u32[]{:S(2)}, u32[]{:S(2)}) collective-permute-start(bf16[192,768]{1,0:T(8,128)(2,1)S(1)} %copy-done.59), channel_id=1, source_target_pairs={{0,2},{1,3},{2,0},{3,1},{4,6},{5,7},{6,4},{7,5},{8,10},{9,11},{10,... | collective-permute-start | bytes 884744 | tf_op jit(solution)/shard_map/ppermute | solution.py:62
  65.1 20.7 %collective-permute-start.16 = (bf16[2,48,3072]{2,1,0:T(8,128)(2,1)}, bf16[2,48,3072]{2,1,0:T(8,128)(2,1)S(1)}, u32[]{:S(2)}, u32[]{:S(2)}) collective-permute-start(bf16[2,48,3072]{2,1,0:T(8,128)(2,1)} %get-tuple-element.133), channel_id=1, source_target_pairs={{0,4},{1,5},{2,6},{3,7},{4,0},{5,1},{6,2},{7,3},{8,12},{9,13},{10,... | collective-permute-start | bytes 1769480 | tf_op jit(solution)/shard_map/ppermute | solution.py:62
  65.8 21.6 %collective-permute-start.15 = (bf16[2,48,3072]{2,1,0:T(8,128)(2,1)}, bf16[2,48,3072]{2,1,0:T(8,128)(2,1)}, u32[]{:S(2)}, u32[]{:S(2)}) collective-permute-start(bf16[2,48,3072]{2,1,0:T(8,128)(2,1)} %get-tuple-element.132), channel_id=1, source_target_pairs={{0,2},{1,3},{2,0},{3,1},{4,6},{5,7},{6,4},{7,5},{8,10},{9,11},{10,... | collective-permute-start | bytes 1769480 | tf_op jit(solution)/shard_map/ppermute | solution.py:62
  68.7 20.2 %collective-permute-start.14 = (bf16[2,2,96,768]{3,2,1,0:T(8,128)(2,1)}, bf16[2,2,96,768]{3,2,1,0:T(8,128)(2,1)}, u32[]{:S(2)}, u32[]{:S(2)}) collective-permute-start(bf16[2,2,96,768]{3,2,1,0:T(8,128)(2,1)} %constant_dynamic-update-slice_fusion.1), channel_id=1, source_target_pairs={{0,1},{1,0},{2,3},{3,2},{4,5},{5,4},{6,7},{7,6},{8,9},{9,8},{10,11... | collective-permute-start | bytes 1769480 | tf_op jit(solution)/shard_map/ppermute | solution.py:62
  90.4 15.8 %collective-permute-start.20 = (bf16[2,192,768]{2,1,0:T(8,128)(2,1)S(1)}, bf16[2,192,768]{2,1,0:T(8,128)(2,1)S(1)}, u32[]{:S(2)}, u32[]{:S(2)}) collective-permute-start(bf16[2,192,768]{2,1,0:T(8,128)(2,1)S(1)} %get-tuple-element.140), channel_id=1, source_target_pairs={{0,2},{1,3},{2,0},{3,1},{4,6},{5,7},{6,4},{7,5},{8,10},{9,11},{10,... | collective-permute-start | bytes 1769480 | tf_op jit(solution)/shard_map/ppermute | solution.py:62
  91.0 15.5 %collective-permute-start.21 = (bf16[2,192,768]{2,1,0:T(8,128)(2,1)S(1)}, bf16[2,192,768]{2,1,0:T(8,128)(2,1)S(1)}, u32[]{:S(2)}, u32[]{:S(2)}) collective-permute-start(bf16[2,192,768]{2,1,0:T(8,128)(2,1)S(1)} %get-tuple-element.141), channel_id=1, source_target_pairs={{0,4},{1,5},{2,6},{3,7},{4,0},{5,1},{6,2},{7,3},{8,12},{9,13},{10,... | collective-permute-start | bytes 1769480 | tf_op jit(solution)/shard_map/ppermute | solution.py:62
  92.6 15.9 %collective-permute-start.19 = (bf16[2,2,96,3072]{3,2,1,0:T(8,128)(2,1)S(1)}, bf16[2,2,96,3072]{3,2,1,0:T(8,128)(2,1)S(1)}, u32[]{:S(2)}, u32[]{:S(2)}) collective-permute-start(bf16[2,2,96,3072]{3,2,1,0:T(8,128)(2,1)S(1)} %constant_dynamic-update-slice_fusion.2), channel_id=1, source_target_pairs={{0,1},{1,0},{2,3},{3,2},{4,5},{5,4},{6,7},{7,6},{8,9},{9,8},{10,11... | collective-permute-start | bytes 7077896 | tf_op jit(solution)/shard_map/ppermute | solution.py:62
  108.4 37.6 %collective-permute-start.22 = (bf16[2,2,384,768]{3,2,1,0:T(8,128)(2,1)}, bf16[2,2,384,768]{3,2,1,0:T(8,128)(2,1)}, u32[]{:S(2)}, u32[]{:S(2)}) collective-permute-start(bf16[2,2,384,768]{3,2,1,0:T(8,128)(2,1)} %maximum_maximum_fusion), channel_id=1, source_target_pairs={{0,1},{1,0},{2,3},{3,2},{4,5},{5,4},{6,7},{7,6},{8,9},{9,8},{10,11... | collective-permute-start | bytes 7077896 | tf_op jit(solution)/shard_map/ppermute | solution.py:62
  161.4 16.5 %collective-permute-start.23 = (bf16[2,2,384,768]{3,2,1,0:T(8,128)(2,1)}, bf16[2,2,384,768]{3,2,1,0:T(8,128)(2,1)}, u32[]{:S(2)}, u32[]{:S(2)}) collective-permute-start(bf16[2,2,384,768]{3,2,1,0:T(8,128)(2,1)} %dynamic-slice_bitcast_fusion.1), channel_id=1, source_target_pairs={{0,1},{1,0},{2,3},{3,2},{4,5},{5,4},{6,7},{7,6},{8,9},{9,8},{10,11... | collective-permute-start | bytes 7077896 | tf_op jit(solution)/shard_map/ppermute | solution.py:62
  180.5 15.4 %collective-permute-start.25 = (bf16[2,192,768]{2,1,0:T(8,128)(2,1)S(1)}, bf16[2,192,768]{2,1,0:T(8,128)(2,1)S(1)}, u32[]{:S(2)}, u32[]{:S(2)}) collective-permute-start(bf16[2,192,768]{2,1,0:T(8,128)(2,1)S(1)} %dynamic-slice_bitcast_fusion.6), channel_id=1, source_target_pairs={{0,4},{1,5},{2,6},{3,7},{4,0},{5,1},{6,2},{7,3},{8,12},{9,13},{10,... | collective-permute-start | bytes 1769480 | tf_op jit(solution)/shard_map/ppermute | solution.py:62
  182.0 15.1 %collective-permute-start.24 = (bf16[2,192,768]{2,1,0:T(8,128)(2,1)S(1)}, bf16[2,192,768]{2,1,0:T(8,128)(2,1)S(1)}, u32[]{:S(2)}, u32[]{:S(2)}) collective-permute-start(bf16[2,192,768]{2,1,0:T(8,128)(2,1)S(1)} %dynamic-slice_bitcast_fusion.7), channel_id=1, source_target_pairs={{0,2},{1,3},{2,0},{3,1},{4,6},{5,7},{6,4},{7,5},{8,10},{9,11},{10,... | collective-permute-start | bytes 1769480 | tf_op jit(solution)/shard_map/ppermute | solution.py:62
  198.9 15.7 %collective-permute-start.28 = (bf16[2,2,96,3072]{3,2,1,0:T(8,128)(2,1)}, bf16[2,2,96,3072]{3,2,1,0:T(8,128)(2,1)}, u32[]{:S(2)}, u32[]{:S(2)}) collective-permute-start(bf16[2,2,96,3072]{3,2,1,0:T(8,128)(2,1)} %dynamic-slice_bitcast_fusion), channel_id=1, source_target_pairs={{0,1},{1,0},{2,3},{3,2},{4,5},{5,4},{6,7},{7,6},{8,9},{9,8},{10,11... | collective-permute-start | bytes 7077896 | tf_op jit(solution)/shard_map/ppermute | solution.py:62
  199.6 12.6 %collective-permute-start.27 = (bf16[192,768]{1,0:T(8,128)(2,1)}, bf16[192,768]{1,0:T(8,128)(2,1)}, u32[]{:S(2)}, u32[]{:S(2)}) collective-permute-start(bf16[192,768]{1,0:T(8,128)(2,1)} %dynamic-slice_bitcast_fusion.12), channel_id=1, source_target_pairs={{0,2},{1,3},{2,0},{3,1},{4,6},{5,7},{6,4},{7,5},{8,10},{9,11},{10,... | collective-permute-start | bytes 884744 | tf_op jit(solution)/shard_map/ppermute | solution.py:62
  201.7 11.7 %collective-permute-start.26 = (bf16[192,768]{1,0:T(8,128)(2,1)}, bf16[192,768]{1,0:T(8,128)(2,1)}, u32[]{:S(2)}, u32[]{:S(2)}) collective-permute-start(bf16[192,768]{1,0:T(8,128)(2,1)} %dynamic-slice_bitcast_fusion.13), channel_id=1, source_target_pairs={{0,4},{1,5},{2,6},{3,7},{4,0},{5,1},{6,2},{7,3},{8,12},{9,13},{10,... | collective-permute-start | bytes 884744 | tf_op jit(solution)/shard_map/ppermute | solution.py:62
  218.1 27.1 %collective-permute-start.32 = (bf16[2,48,3072]{2,1,0:T(8,128)(2,1)S(1)}, bf16[2,48,3072]{2,1,0:T(8,128)(2,1)S(1)}, u32[]{:S(2)}, u32[]{:S(2)}) collective-permute-start(bf16[2,48,3072]{2,1,0:T(8,128)(2,1)S(1)} %dynamic-slice_bitcast_fusion.4), channel_id=1, source_target_pairs={{0,4},{1,5},{2,6},{3,7},{4,0},{5,1},{6,2},{7,3},{8,12},{9,13},{10,... | collective-permute-start | bytes 1769480 | tf_op jit(solution)/shard_map/ppermute | solution.py:62
  219.6 25.8 %collective-permute-start.31 = (bf16[2,48,3072]{2,1,0:T(8,128)(2,1)S(1)}, bf16[2,48,3072]{2,1,0:T(8,128)(2,1)S(1)}, u32[]{:S(2)}, u32[]{:S(2)}) collective-permute-start(bf16[2,48,3072]{2,1,0:T(8,128)(2,1)S(1)} %dynamic-slice_bitcast_fusion.5), channel_id=1, source_target_pairs={{0,2},{1,3},{2,0},{3,1},{4,6},{5,7},{6,4},{7,5},{8,10},{9,11},{10,... | collective-permute-start | bytes 1769480 | tf_op jit(solution)/shard_map/ppermute | solution.py:62
  220.3 24.6 %collective-permute-start.30 = (bf16[192,768]{1,0:T(8,128)(2,1)S(1)}, bf16[192,768]{1,0:T(8,128)(2,1)S(1)}, u32[]{:S(2)}, u32[]{:S(2)}) collective-permute-start(bf16[192,768]{1,0:T(8,128)(2,1)S(1)} %fusion.29), channel_id=1, source_target_pairs={{0,8},{24,16},{1,9},{25,17},{2,10},{26,18},{3,11},{27,19},{4,12},{... | collective-permute-start | bytes 884744 | tf_op jit(solution)/shard_map/ppermute | solution.py:156
  223.9 21.1 %collective-permute-start.29 = (bf16[192,768]{1,0:T(8,128)(2,1)S(1)}, bf16[192,768]{1,0:T(8,128)(2,1)S(1)}, u32[]{:S(2)}, u32[]{:S(2)}) collective-permute-start(bf16[192,768]{1,0:T(8,128)(2,1)S(1)} %fusion.30), channel_id=1, source_target_pairs={{0,8},{24,16},{1,9},{25,17},{2,10},{26,18},{3,11},{27,19},{4,12},{... | collective-permute-start | bytes 884744 | tf_op jit(solution)/shard_map/ppermute | solution.py:156
  245.6 12.1 %collective-permute-start.37 = (bf16[2,2,96,768]{3,2,1,0:T(8,128)(2,1)S(1)}, bf16[2,2,96,768]{3,2,1,0:T(8,128)(2,1)S(1)}, u32[]{:S(2)}, u32[]{:S(2)}) collective-permute-start(bf16[2,2,96,768]{3,2,1,0:T(8,128)(2,1)S(1)} %dynamic-slice_bitcast_fusion.3), channel_id=1, source_target_pairs={{0,1},{1,0},{2,3},{3,2},{4,5},{5,4},{6,7},{7,6},{8,9},{9,8},{10,11... | collective-permute-start | bytes 1769480 | tf_op jit(solution)/shard_map/ppermute | solution.py:62
  259.2 46.4 %collective-permute-start.44 = (bf16[2,2,96,2304]{3,2,1,0:T(8,128)(2,1)}, bf16[2,2,96,2304]{3,2,1,0:T(8,128)(2,1)}, u32[]{:S(2)}, u32[]{:S(2)}) collective-permute-start(bf16[2,2,96,2304]{3,2,1,0:T(8,128)(2,1)} %dynamic-slice_bitcast_fusion.2), channel_id=1, source_target_pairs={{0,1},{1,0},{2,3},{3,2},{4,5},{5,4},{6,7},{7,6},{8,9},{9,8},{10,11... | collective-permute-start | bytes 5308424 | tf_op jit(solution)/shard_map/ppermute | solution.py:62
  260.0 26.4 %collective-permute-start.43 = (bf16[2,48,768]{2,1,0:T(8,128)(2,1)}, bf16[2,48,768]{2,1,0:T(8,128)(2,1)}, u32[]{:S(2)}, u32[]{:S(2)}) collective-permute-start(bf16[2,48,768]{2,1,0:T(8,128)(2,1)} %dynamic-slice_bitcast_fusion.16), channel_id=1, source_target_pairs={{0,4},{1,5},{2,6},{3,7},{4,0},{5,1},{6,2},{7,3},{8,12},{9,13},{10,... | collective-permute-start | bytes 442376 | tf_op jit(solution)/shard_map/ppermute | solution.py:62
  261.5 28.1 %collective-permute-start.42 = (bf16[2,48,768]{2,1,0:T(8,128)(2,1)}, bf16[2,48,768]{2,1,0:T(8,128)(2,1)}, u32[]{:S(2)}, u32[]{:S(2)}) collective-permute-start(bf16[2,48,768]{2,1,0:T(8,128)(2,1)} %dynamic-slice_bitcast_fusion.17), channel_id=1, source_target_pairs={{0,2},{1,3},{2,0},{3,1},{4,6},{5,7},{6,4},{7,5},{8,10},{9,11},{10,... | collective-permute-start | bytes 442376 | tf_op jit(solution)/shard_map/ppermute | solution.py:62
  262.9 29.7 %collective-permute-start.41 = (bf16[48,3072]{1,0:T(8,128)(2,1)S(1)}, bf16[48,3072]{1,0:T(8,128)(2,1)}, u32[]{:S(2)}, u32[]{:S(2)}) collective-permute-start(bf16[48,3072]{1,0:T(8,128)(2,1)S(1)} %fusion.27), channel_id=1, source_target_pairs={{0,8},{24,16},{1,9},{25,17},{2,10},{26,18},{3,11},{27,19},{4,12},{... | collective-permute-start | bytes 884744 | tf_op jit(solution)/shard_map/ppermute | solution.py:156
  273.6 30.8 %collective-permute-start.40 = (bf16[48,3072]{1,0:T(8,128)(2,1)}, bf16[48,3072]{1,0:T(8,128)(2,1)}, u32[]{:S(2)}, u32[]{:S(2)}) collective-permute-start(bf16[48,3072]{1,0:T(8,128)(2,1)} %fusion.28), channel_id=1, source_target_pairs={{0,8},{24,16},{1,9},{25,17},{2,10},{26,18},{3,11},{27,19},{4,12},{... | collective-permute-start | bytes 884744 | tf_op jit(solution)/shard_map/ppermute | solution.py:156
  286.4 12.3 %collective-permute-start.39 = (bf16[192,768]{1,0:T(8,128)(2,1)}, bf16[192,768]{1,0:T(8,128)(2,1)S(1)}, u32[]{:S(2)}, u32[]{:S(2)}) collective-permute-start(bf16[192,768]{1,0:T(8,128)(2,1)} %add_convert_fusion.7), channel_id=1, source_target_pairs={{8,0},{16,24},{9,1},{17,25},{10,2},{18,26},{11,3},{19,27},{12,4},{... | collective-permute-start | bytes 884744 | tf_op jit(solution)/shard_map/ppermute | solution.py:163
  289.6 14.1 %collective-permute-start.38 = (bf16[192,768]{1,0:T(8,128)(2,1)}, bf16[192,768]{1,0:T(8,128)(2,1)S(1)}, u32[]{:S(2)}, u32[]{:S(2)}) collective-permute-start(bf16[192,768]{1,0:T(8,128)(2,1)} %add_convert_fusion.8), channel_id=1, source_target_pairs={{8,0},{16,24},{9,1},{17,25},{10,2},{18,26},{11,3},{19,27},{12,4},{... | collective-permute-start | bytes 884744 | tf_op jit(solution)/shard_map/ppermute | solution.py:163
  309.8 16.3 %collective-permute-start.51 = (f32[2,2,12,96]{3,1,2,0:T(2,128)S(1)}, f32[2,2,12,96]{3,1,2,0:T(2,128)S(1)}, u32[]{:S(2)}, u32[]{:S(2)}) collective-permute-start(f32[2,2,12,96]{3,1,2,0:T(2,128)S(1)} %bitcast.309), channel_id=1, source_target_pairs={{0,1},{1,0},{2,3},{3,2},{4,5},{5,4},{6,7},{7,6},{8,9},{9,8},{10,11... | collective-permute-start | bytes 55304 | tf_op jit(solution)/shard_map/ppermute | solution.py:62
  311.5 16.2 %collective-permute-start.50 = (bf16[2,48,2304]{2,1,0:T(8,128)(2,1)S(1)}, bf16[2,48,2304]{2,1,0:T(8,128)(2,1)S(1)}, u32[]{:S(2)}, u32[]{:S(2)}) collective-permute-start(bf16[2,48,2304]{2,1,0:T(8,128)(2,1)S(1)} %dynamic-slice_bitcast_fusion.8), channel_id=1, source_target_pairs={{0,4},{1,5},{2,6},{3,7},{4,0},{5,1},{6,2},{7,3},{8,12},{9,13},{10,... | collective-permute-start | bytes 1327112 | tf_op jit(solution)/shard_map/ppermute | solution.py:62
  312.2 15.6 %collective-permute-start.49 = (bf16[2,48,2304]{2,1,0:T(8,128)(2,1)S(1)}, bf16[2,48,2304]{2,1,0:T(8,128)(2,1)S(1)}, u32[]{:S(2)}, u32[]{:S(2)}) collective-permute-start(bf16[2,48,2304]{2,1,0:T(8,128)(2,1)S(1)} %dynamic-slice_bitcast_fusion.9), channel_id=1, source_target_pairs={{0,2},{1,3},{2,0},{3,1},{4,6},{5,7},{6,4},{7,5},{8,10},{9,11},{10,... | collective-permute-start | bytes 1327112 | tf_op jit(solution)/shard_map/ppermute | solution.py:62
  313.5 13.2 %collective-permute-start.48 = (bf16[48,768]{1,0:T(8,128)(2,1)S(1)}, bf16[48,768]{1,0:T(8,128)(2,1)S(1)}, u32[]{:S(2)}, u32[]{:S(2)}) collective-permute-start(bf16[48,768]{1,0:T(8,128)(2,1)S(1)} %dynamic-slice_bitcast_fusion.18), channel_id=1, source_target_pairs={{0,2},{1,3},{2,0},{3,1},{4,6},{5,7},{6,4},{7,5},{8,10},{9,11},{10,... | collective-permute-start | bytes 221192 | tf_op jit(solution)/shard_map/ppermute | solution.py:62
  314.4 13.1 %collective-permute-start.47 = (bf16[48,768]{1,0:T(8,128)(2,1)S(1)}, bf16[48,768]{1,0:T(8,128)(2,1)S(1)}, u32[]{:S(2)}, u32[]{:S(2)}) collective-permute-start(bf16[48,768]{1,0:T(8,128)(2,1)S(1)} %dynamic-slice_bitcast_fusion.19), channel_id=1, source_target_pairs={{0,4},{1,5},{2,6},{3,7},{4,0},{5,1},{6,2},{7,3},{8,12},{9,13},{10,... | collective-permute-start | bytes 221192 | tf_op jit(solution)/shard_map/ppermute | solution.py:62
  328.0 21.6 %collective-permute-start.58 = (f32[2,12,96]{2,0,1:T(2,128)S(1)}, f32[2,12,96]{2,0,1:T(2,128)S(1)}, u32[]{:S(2)}, u32[]{:S(2)}) collective-permute-start(f32[2,12,96]{2,0,1:T(2,128)S(1)} %bitcast.310), channel_id=1, source_target_pairs={{0,2},{1,3},{2,0},{3,1},{4,6},{5,7},{6,4},{7,5},{8,10},{9,11},{10,... | collective-permute-start | bytes 27656 | tf_op jit(solution)/shard_map/ppermute | solution.py:62
  329.3 23.1 %collective-permute-start.57 = (bf16[48,2304]{1,0:T(8,128)(2,1)S(1)}, bf16[48,2304]{1,0:T(8,128)(2,1)S(1)}, u32[]{:S(2)}, u32[]{:S(2)}) collective-permute-start(bf16[48,2304]{1,0:T(8,128)(2,1)S(1)} %dynamic-slice_bitcast_fusion.14), channel_id=1, source_target_pairs={{0,2},{1,3},{2,0},{3,1},{4,6},{5,7},{6,4},{7,5},{8,10},{9,11},{10,... | collective-permute-start | bytes 663560 | tf_op jit(solution)/shard_map/ppermute | solution.py:62
  330.2 22.3 %collective-permute-start.56 = (bf16[48,2304]{1,0:T(8,128)(2,1)S(1)}, bf16[48,2304]{1,0:T(8,128)(2,1)S(1)}, u32[]{:S(2)}, u32[]{:S(2)}) collective-permute-start(bf16[48,2304]{1,0:T(8,128)(2,1)S(1)} %dynamic-slice_bitcast_fusion.15), channel_id=1, source_target_pairs={{0,4},{1,5},{2,6},{3,7},{4,0},{5,1},{6,2},{7,3},{8,12},{9,13},{10,... | collective-permute-start | bytes 663560 | tf_op jit(solution)/shard_map/ppermute | solution.py:62
  331.1 19.9 %collective-permute-start.55 = (bf16[48,768]{1,0:T(8,128)(2,1)S(1)}, bf16[48,768]{1,0:T(8,128)(2,1)S(1)}, u32[]{:S(2)}, u32[]{:S(2)}) collective-permute-start(bf16[48,768]{1,0:T(8,128)(2,1)S(1)} %fusion.36), channel_id=1, source_target_pairs={{0,8},{24,16},{1,9},{25,17},{2,10},{26,18},{3,11},{27,19},{4,12},{... | collective-permute-start | bytes 221192 | tf_op jit(solution)/shard_map/ppermute | solution.py:156
  351.0 13.1 %collective-permute-start.52 = (bf16[48,3072]{1,0:T(8,128)(2,1)S(1)}, bf16[48,3072]{1,0:T(8,128)(2,1)S(1)}, u32[]{:S(2)}, u32[]{:S(2)}) collective-permute-start(bf16[48,3072]{1,0:T(8,128)(2,1)S(1)} %add_convert_fusion.4), channel_id=1, source_target_pairs={{8,0},{16,24},{9,1},{17,25},{10,2},{18,26},{11,3},{19,27},{12,4},{... | collective-permute-start | bytes 884744 | tf_op jit(solution)/shard_map/ppermute | solution.py:163
  372.9 13.3 %collective-permute-start.68 = (f32[12,96]{1,0:T(8,128)S(1)}, f32[12,96]{1,0:T(8,128)S(1)}, u32[]{:S(2)}, u32[]{:S(2)}) collective-permute-start(f32[12,96]{1,0:T(8,128)S(1)} %bitcast_add_fusion.2), channel_id=1, source_target_pairs={{0,8},{24,16},{1,9},{25,17},{2,10},{26,18},{3,11},{27,19},{4,12},{... | collective-permute-start | bytes 13832 | tf_op jit(solution)/shard_map/ppermute | solution.py:156
  383.5 12.9 %collective-permute-start.67 = (bf16[48,2304]{1,0:T(8,128)(2,1)S(1)}, bf16[48,2304]{1,0:T(8,128)(2,1)S(1)}, u32[]{:S(2)}, u32[]{:S(2)}) collective-permute-start(bf16[48,2304]{1,0:T(8,128)(2,1)S(1)} %add_convert_fusion.13), channel_id=1, source_target_pairs={{8,16},{16,8},{9,17},{17,9},{10,18},{18,10},{11,19},{19,11},{12,20... | collective-permute-start | bytes 663560 | tf_op jit(solution)/shard_map/ppermute | solution.py:158
  384.2 12.3 %collective-permute-start.66 = (bf16[48,2304]{1,0:T(8,128)(2,1)S(1)}, bf16[48,2304]{1,0:T(8,128)(2,1)S(1)}, u32[]{:S(2)}, u32[]{:S(2)}) collective-permute-start(bf16[48,2304]{1,0:T(8,128)(2,1)S(1)} %add_convert_fusion.14), channel_id=1, source_target_pairs={{8,16},{16,8},{9,17},{17,9},{10,18},{18,10},{11,19},{19,11},{12,20... | collective-permute-start | bytes 663560 | tf_op jit(solution)/shard_map/ppermute | solution.py:158
  384.9 11.5 %collective-permute-start.64 = (bf16[48,768]{1,0:T(8,128)(2,1)S(1)}, bf16[48,768]{1,0:T(8,128)(2,1)S(1)}, u32[]{:S(2)}, u32[]{:S(2)}) collective-permute-start(bf16[48,768]{1,0:T(8,128)(2,1)S(1)} %add_convert_fusion.18), channel_id=1, source_target_pairs={{8,0},{16,24},{9,1},{17,25},{10,2},{18,26},{11,3},{19,27},{12,4},{... | collective-permute-start | bytes 221192 | tf_op jit(solution)/shard_map/ppermute | solution.py:163
  (112 other events, 1145.3 us)
